TPU v7x, 512 devices: a whole 4x4x16 slice. The times are simulated.
512 devices in a mesh: tm: 16 (over y, x), space: 8 (over z_hi, core), dp: 4 (over z_lo).
Axes of the slice: x: 4, y: 4, z: 16 (z_hi: 4, z_lo: 4; z = z_hi * 4 + z_lo), core: 2. Of those that a mesh axis runs over, the one named last changes fastest.
Arguments:
- projected: bfloat16 [64, 1024, 3, 40, 128], P(('dp', 'tm'), None, None, 'space'), parts along dimension 0, may hold values from -256 to 256
- q_gain: float32 [40, 128], P('space'), may hold values from 0.1 to 1.9
- k_gain: float32 [40, 128], P('space'), may hold values from 0.1 to 1.9
- head_weight: float32 [40, 128], P('space'), may hold values from -0.078125 to 0.078125
- step_scale: float32 [4, 40, 128], P(None, 'space'), may hold values from 0.5 to 1.5
- timestep: int32 [64], P('dp'), parts along dimension 0, may hold values from 0 to 3
- frame_count: int32 [4096], P('dp'), parts along dimension 0, may hold values from 1 to 16
Outputs:
- logits: float32 [64, 1024], P(('dp', 'tm'), 'space'), parts along dimension 0
There are 4 independent parts, one for each index of `dp`. A program takes and returns all parts, laid end to end along the dimension named above; an argument that names none is the same for every part. Nothing has to cross between parts.
All inputs are finite; a program needn't handle non-finite values.
Results may differ from a plain program's by a relative error of at most 0.01.
Values may be sent and summed in bfloat16 or wider, within the bound.
A program may use at most 64 MiB of HBM per device.

v0:
```python
import jax
import jax.numpy as jnp
from jax import lax
from jax.sharding import PartitionSpec as P

HEADS = 40
HEAD = 128


epsilon = 1e-06


def on_device(projected, q_gain, k_gain, head_weight, step_scale, timestep, frame_count):
    channels = HEADS * HEAD
    scaling = HEAD ** (-0.5)
    shard_rows = projected[0]
    queries = shard_rows[:, 0]
    key_rows = shard_rows[:, 1]
    values = shard_rows[:, 2]
    query_sums = jnp.sum(jnp.square(queries.astype(jnp.float32)), axis=(1, 2))
    key_sums = jnp.sum(jnp.square(key_rows.astype(jnp.float32)), axis=(1, 2))
    query_total, key_total = lax.psum((query_sums, key_sums), "space")

    def normalize(features_in, sum_squares, gain_row):
        factor = lax.rsqrt(sum_squares / channels + epsilon)
        scaled = (features_in.astype(jnp.float32) * factor[:, None, None] * gain_row).astype(
            jnp.bfloat16
        )
        return jnp.transpose(scaled, (1, 0, 2))

    q_heads = normalize(queries, query_total, q_gain)
    k_heads = normalize(key_rows, key_total, k_gain)

    def one_head(head_index):
        query_head = lax.dynamic_index_in_dim(q_heads, head_index, 0, keepdims=False)
        key_head = lax.dynamic_index_in_dim(k_heads, head_index, 0, keepdims=False)
        value_head = lax.dynamic_index_in_dim(values, head_index, 1, keepdims=False)
        scores = (
            lax.dot_general(
                query_head, key_head, (((1,), (1,)), ((), ())), preferred_element_type=jnp.float32
            )
            * scaling
        )
        row_max = jnp.max(scores, axis=1, keepdims=True)
        exponent = jnp.exp(scores - row_max)
        weights = (exponent / jnp.sum(exponent, axis=1, keepdims=True)).astype(jnp.bfloat16)
        return jnp.dot(weights, value_head, preferred_element_type=jnp.float32).astype(jnp.bfloat16)

    spatial_out = lax.optimization_barrier(lax.map(one_head, jnp.arange(q_heads.shape[0])))
    query_far = lax.all_to_all(q_heads[:, None], "tm", split_axis=2, concat_axis=1, tiled=True)
    key_far = lax.all_to_all(k_heads[:, None], "tm", split_axis=2, concat_axis=1, tiled=True)
    spatial_far = lax.all_to_all(
        spatial_out[:, None], "tm", split_axis=2, concat_axis=1, tiled=True
    )
    block = query_far.shape[2]
    block_counts = lax.dynamic_slice_in_dim(frame_count, lax.axis_index("tm") * block, block)
    scores = (
        jnp.einsum("hfpe,hgpe->hpfg", query_far, key_far, preferred_element_type=jnp.float32)
        * scaling
    )
    live_frames = jnp.arange(query_far.shape[1], dtype=jnp.int32)[None, :] < block_counts[:, None]
    scores = jnp.where(live_frames[None, :, None, :], scores, -1e30)
    row_max = jnp.max(scores, axis=3, keepdims=True)
    exponent = jnp.exp(scores - row_max)
    weights = (exponent / jnp.sum(exponent, axis=3, keepdims=True)).astype(jnp.bfloat16)
    temporal_mix = jnp.einsum(
        "hpfg,hgpe->hfpe", weights, spatial_far, preferred_element_type=jnp.float32
    ).astype(jnp.bfloat16)
    temporal_mix, spatial_far = (lax.optimization_barrier(temporal_mix), spatial_far)
    own_step = lax.dynamic_index_in_dim(timestep, lax.axis_index("tm"), 0, keepdims=False)
    row_scale = lax.dynamic_index_in_dim(step_scale, own_step, 0, keepdims=False)
    mixed_home = lax.all_to_all(temporal_mix, "tm", split_axis=1, concat_axis=2, tiled=True)
    combined = spatial_out.astype(jnp.float32) + mixed_home[:, 0].astype(jnp.float32)
    modulated = combined * row_scale[:, None, :]
    dot_home = jnp.sum(modulated * head_weight[:, None, :], axis=(0, 2))
    square_home = jnp.sum(modulated * modulated, axis=(0, 2))
    dot_mine, square_mine = (
        lax.psum_scatter(dot_home, "space", scatter_dimension=0, tiled=True),
        lax.psum_scatter(square_home, "space", scatter_dimension=0, tiled=True),
    )
    logits = dot_mine * lax.rsqrt(square_mine / channels + epsilon)
    return logits[None, :]


def solution(mesh):
    in_specs = (
        P(("dp", "tm"), None, None, "space", None),
        P("space", None),
        P("space", None),
        P("space", None),
        P(None, "space", None),
        P("dp"),
        P("dp"),
    )
    out_specs = P(("dp", "tm"), "space")
    return jax.shard_map(
        on_device, mesh=mesh, in_specs=in_specs, out_specs=out_specs, check_vma=False
    )
```

profile of v0, /device:TPU:1, one launch (start us, length us, event | category | flops | bytes accessed | tf_op | source)
XLA Modules:
  0.0 206.2 jit_solution(14934503177007581854)
XLA Ops:
  0.0 5.0 %copy.59 = bf16[1,1024,3,5,128]{4,3,1,2,0:T(8,128)(2,1)S(1)} copy(bf16[1,1024,3,5,128]{4,1,3,2,0:T(8,128)(2,1)} %param.9) | data formatting | bytes 7864320 | tf_op args[0]
  5.0 2.6 %copy-done.1 = bf16[1,1024,3,5,128]{4,3,1,2,0:T(8,128)(2,1)} copy-done((bf16[1,1024,3,5,128]{4,3,1,2,0:T(8,128)(2,1)}, bf16[1,1024,3,5,128]{4,3,1,2,0:T(8,128)(2,1)S(1)}, u32[]{:S(2)}) %copy-start.1) | copy-done | bytes 3932184
  7.6 4.5 %fusion.19 = (f32[1024]{0:T(1024)S(1)}, f32[1024]{0:T(1024)S(1)}) fusion(bf16[1024,3,5,128]{3,2,0,1:T(8,128)(2,1)S(1)} %bitcast.86), kind=kLoop, calls=%fused_computation.27 | loop fusion | flops 3930112 | bytes 2629632 | tf_op jit(solution)/shard_map/reduce_sum | solution.py:21
  12.1 24.3 %all-reduce.3 = (f32[1024]{0:T(1024)S(1)}, f32[1024]{0:T(1024)S(1)}) all-reduce(f32[1024]{0:T(1024)S(1)} %get-tuple-element.51, f32[1024]{0:T(1024)S(1)} %get-tuple-element.50), channel_id=1, replica_groups=mesh['tm'=16,'space'=8,'dp'=4] {'space'}, use_global_device_ids=true, to_apply=%region_1.0 | all-reduce | flops 2048 | bytes 16384 | tf_op jit(solution)/shard_map/psum | solution.py:22
  36.4 7.7 %fusion.35 = (bf16[5,1,1024,128]{3,0,1,2:T(8,128)(2,1)}, bf16[5,1024,128]{2,0,1:T(8,128)(2,1)}, bf16[5,1024,128]{2,0,1:T(8,128)(2,1)S(1)}, bf16[5,1,1024,128]{3,0,1,2:T(8,128)(2,1)}) fusion(f32[5,128]{1,0:T(8,128)S(1)} %copy-done.5, f32[1024]{0:T(1024)S(1)} %get-tuple-element.81, bf16[1024,3,5,128]{3,2,0,1:T(8,128)(2,1)} %bitcast.87, ...), kind=kLoop, calls=%fused_computation.54 | loop fusion | flops 5242880 | bytes 7877632 | tf_op jit(solution)/shard_map/broadcast_in_dim | solution.py:50
  44.1 6.8 %all-to-all-start.2 = ((bf16[5,1,1024,128]{3,0,1,2:T(8,128)(2,1)}), bf16[5,1,1024,128]{3,0,1,2:T(8,128)(2,1)}, u32[]{:S(2)}, u32[]{:S(2)}) async-start(bf16[5,1,1024,128]{3,0,1,2:T(8,128)(2,1)} %get-tuple-element.77), calls=%async_computation.2 | async-start | bytes 4194304 | tf_op jit(solution)/shard_map/all_to_all | solution.py:51
  50.9 1.8 copy.19
  52.6 1.3 copy.20
  54.0 2.0 slice_bitcast_fusion
  55.9 1.3 copy.21
  57.2 17.5 %all-to-all-done.2 = bf16[5,1,1024,128]{3,0,1,2:T(8,128)(2,1)} async-done(((bf16[5,1,1024,128]{3,0,1,2:T(8,128)(2,1)}), bf16[5,1,1024,128]{3,0,1,2:T(8,128)(2,1)}, u32[]{:S(2)}, u32[]{:S(2)}) %all-to-all-start.2) | async-done | bytes 1310752 | tf_op jit(solution)/shard_map/all_to_all | solution.py:51
  74.7 5.0 %all-to-all-start.1 = ((bf16[5,1,1024,128]{3,0,1,2:T(8,128)(2,1)}), bf16[5,1,1024,128]{3,0,1,2:T(8,128)(2,1)}, u32[]{:S(2)}, u32[]{:S(2)}) async-start(bf16[5,1,1024,128]{3,0,1,2:T(8,128)(2,1)} %get-tuple-element.72), calls=%async_computation.1 | async-start | bytes 4194304 | tf_op jit(solution)/shard_map/all_to_all | solution.py:50
  79.8 35.4 %while.10 = (s32[]{:T(128)}, bf16[5,1024,128]{2,1,0:T(8,128)(2,1)S(1)}, s32[5]{0:T(128)S(1)}, bf16[5,1024,128]{2,1,0:T(8,128)(2,1)S(1)}, bf16[5,1024,128]{2,1,0:...) while((s32[]{:T(128)}, bf16[5,1024,128]{2,1,0:T(8,128)(2,1)S(1)}, ...), condition=%wide.region_7.8_spmd, body=%wide.region_4.7_spmd.sunk | while | flops 546437120 | bytes 13653147 | solution.py:49
  82.2 1.7 multiply_reduce_fusion.4
  84.6 2.2 %fusion.55 = bf16[5,1024,128]{2,1,0:T(8,128)(2,1)S(1)} fusion(bf16[5,1024,128]{2,1,0:T(8,128)(2,1)S(1)} %get-tuple-element.133, s32[]{:T(128)S(6)} %copy.65, f32[1024,1024]{0,1:T(8,128)S(1)} %get-tuple-element.121, f32[1024]{0:T(1024)S(1)} %fusion.54, f32[1024]{0:T(1024)S(1)} %get-tuple-element.122, bf16[1024,5,128]{2,0,1:T(8,128)(2,1)} %get-tuple-element.146, ...), kind=kOutput, calls=%fused_computation.7.clone.1 | convolution fusion | flops 272760832 | bytes 4726792 | tf_op jit(solution)/shard_map/while/body/eval_jaxpr/dot_general | solution.py:47
  89.3 1.7 multiply_reduce_fusion.4
  91.7 2.2 %fusion.55 = bf16[5,1024,128]{2,1,0:T(8,128)(2,1)S(1)} fusion(bf16[5,1024,128]{2,1,0:T(8,128)(2,1)S(1)} %get-tuple-element.133, s32[]{:T(128)S(6)} %copy.65, f32[1024,1024]{0,1:T(8,128)S(1)} %get-tuple-element.121, f32[1024]{0:T(1024)S(1)} %fusion.54, f32[1024]{0:T(1024)S(1)} %get-tuple-element.122, bf16[1024,5,128]{2,0,1:T(8,128)(2,1)} %get-tuple-element.146, ...), kind=kOutput, calls=%fused_computation.7.clone.1 | convolution fusion | flops 272760832 | bytes 4726792 | tf_op jit(solution)/shard_map/while/body/eval_jaxpr/dot_general | solution.py:47
  96.4 1.7 multiply_reduce_fusion.4
  98.8 2.2 %fusion.55 = bf16[5,1024,128]{2,1,0:T(8,128)(2,1)S(1)} fusion(bf16[5,1024,128]{2,1,0:T(8,128)(2,1)S(1)} %get-tuple-element.133, s32[]{:T(128)S(6)} %copy.65, f32[1024,1024]{0,1:T(8,128)S(1)} %get-tuple-element.121, f32[1024]{0:T(1024)S(1)} %fusion.54, f32[1024]{0:T(1024)S(1)} %get-tuple-element.122, bf16[1024,5,128]{2,0,1:T(8,128)(2,1)} %get-tuple-element.146, ...), kind=kOutput, calls=%fused_computation.7.clone.1 | convolution fusion | flops 272760832 | bytes 4726792 | tf_op jit(solution)/shard_map/while/body/eval_jaxpr/dot_general | solution.py:47
  103.5 1.7 multiply_reduce_fusion.4
  105.9 2.2 %fusion.55 = bf16[5,1024,128]{2,1,0:T(8,128)(2,1)S(1)} fusion(bf16[5,1024,128]{2,1,0:T(8,128)(2,1)S(1)} %get-tuple-element.133, s32[]{:T(128)S(6)} %copy.65, f32[1024,1024]{0,1:T(8,128)S(1)} %get-tuple-element.121, f32[1024]{0:T(1024)S(1)} %fusion.54, f32[1024]{0:T(1024)S(1)} %get-tuple-element.122, bf16[1024,5,128]{2,0,1:T(8,128)(2,1)} %get-tuple-element.146, ...), kind=kOutput, calls=%fused_computation.7.clone.1 | convolution fusion | flops 272760832 | bytes 4726792 | tf_op jit(solution)/shard_map/while/body/eval_jaxpr/dot_general | solution.py:47
  110.6 1.7 multiply_reduce_fusion.4
  113.0 2.2 %fusion.55 = bf16[5,1024,128]{2,1,0:T(8,128)(2,1)S(1)} fusion(bf16[5,1024,128]{2,1,0:T(8,128)(2,1)S(1)} %get-tuple-element.133, s32[]{:T(128)S(6)} %copy.65, f32[1024,1024]{0,1:T(8,128)S(1)} %get-tuple-element.121, f32[1024]{0:T(1024)S(1)} %fusion.54, f32[1024]{0:T(1024)S(1)} %get-tuple-element.122, bf16[1024,5,128]{2,0,1:T(8,128)(2,1)} %get-tuple-element.146, ...), kind=kOutput, calls=%fused_computation.7.clone.1 | convolution fusion | flops 272760832 | bytes 4726792 | tf_op jit(solution)/shard_map/while/body/eval_jaxpr/dot_general | solution.py:47
  115.2 2.2 %copy.60 = bf16[5,1024,128]{2,0,1:T(8,128)(2,1)} copy(bf16[5,1024,128]{2,1,0:T(8,128)(2,1)S(1)} %get-tuple-element.37) | data formatting | bytes 2621440 | tf_op jit(solution)/shard_map/optimization_barrier | solution.py:49
  117.4 6.6 %all-to-all-start = ((bf16[5,1,1024,128]{3,0,1,2:T(8,128)(2,1)}), bf16[5,1,1024,128]{3,0,1,2:T(8,128)(2,1)S(1)}, u32[]{:S(2)}, u32[]{:S(2)}) async-start(bf16[5,1,1024,128]{3,0,1,2:T(8,128)(2,1)} %bitcast.74), calls=%async_computation | async-start | bytes 4194304 | tf_op jit(solution)/shard_map/all_to_all | solution.py:52
  124.9 7.7 %fusion.41 = (f32[5,64,16]{2,1,0:T(8,128)S(1)}, f32[5,64,16,16]{2,3,1,0:T(8,128)}) fusion(pred[64,16]{1,0:T(8,128)(4,1)S(1)} %iota_compare_fusion, bf16[5,16,64,128]{3,0,2,1:T(8,128)(2,1)} %bitcast.19, bf16[5,16,64,128]{3,0,2,1:T(8,128)(2,1)} %bitcast.16), kind=kOutput, calls=%fused_computation.67 | convolution fusion | flops 21299216 | bytes 2970624 | tf_op jit(solution)/shard_map/sub | solution.py:64
  132.5 14.2 %all-to-all-done = bf16[5,1,1024,128]{3,0,1,2:T(8,128)(2,1)S(1)} async-done(((bf16[5,1,1024,128]{3,0,1,2:T(8,128)(2,1)}), bf16[5,1,1024,128]{3,0,1,2:T(8,128)(2,1)S(1)}, u32[]{:S(2)}, u32[]{:S(2)}) %all-to-all-start) | async-done | bytes 1310752 | tf_op jit(solution)/shard_map/all_to_all | solution.py:52
  146.7 3.6 %fusion.24 = bf16[5,16,64,128]{3,1,2,0:T(8,128)(2,1)S(1)} fusion(f32[5,64,16,16]{2,3,1,0:T(8,128)} %get-tuple-element.79, bf16[5,16,64,128]{3,0,2,1:T(8,128)(2,1)S(1)} %bitcast.89, f32[5,64,16]{2,1,0:T(8,128)S(1)} %get-tuple-element.78), kind=kOutput, calls=%fused_computation.43 | convolution fusion | flops 21790720 | bytes 2969600 | tf_op jit(solution)/shard_map/hpfg,hgpe->hfpe/dot_general | solution.py:66
  150.3 1.4 copy.31
  151.7 5.5 %all-to-all-start.3 = ((bf16[5,16,64,128]{3,2,0,1:T(8,128)(2,1)}), bf16[5,16,64,128]{3,2,0,1:T(8,128)(2,1)S(1)}, u32[]{:S(2)}, u32[]{:S(2)}) async-start(bf16[5,16,64,128]{3,2,0,1:T(8,128)(2,1)} %copy.31), calls=%async_computation.3 | async-start | bytes 2621440 | tf_op jit(solution)/shard_map/all_to_all | solution.py:72
  161.8 9.8 %all-to-all-done.3 = bf16[5,16,64,128]{3,2,0,1:T(8,128)(2,1)S(1)} async-done(((bf16[5,16,64,128]{3,2,0,1:T(8,128)(2,1)}), bf16[5,16,64,128]{3,2,0,1:T(8,128)(2,1)S(1)}, u32[]{:S(2)}, u32[]{:S(2)}) %all-to-all-start.3) | async-done | bytes 1310752 | tf_op jit(solution)/shard_map/all_to_all | solution.py:72
  172.6 33.0 %all-reduce.2 = (f32[1024]{0:T(1024)S(1)}, f32[1024]{0:T(1024)S(1)}) all-reduce(f32[1024]{0:T(1024)S(1)} %get-tuple-element.53, f32[1024]{0:T(1024)S(1)} %get-tuple-element.52), channel_id=2, replica_groups=mesh['tm'=16,'space'=8,'dp'=4] {'space'}, use_global_device_ids=true, to_apply=%region_11.12.clone | all-reduce | flops 2048 | bytes 16384
  (40 shorter events, 11.0 us)
Async XLA Ops:
  0.0 159.8 %copy-start = (f32[4,5,128]{2,0,1:T(4,128)S(1)}, f32[4,5,128]{2,0,1:T(4,128)}, u32[]{:S(2)}) copy-start(f32[4,5,128]{2,0,1:T(4,128)} %param.13) | copy-start | bytes 30724
  5.0 2.7 %copy-start.1 = (bf16[1,1024,3,5,128]{4,3,1,2,0:T(8,128)(2,1)}, bf16[1,1024,3,5,128]{4,3,1,2,0:T(8,128)(2,1)S(1)}, u32[]{:S(2)}) copy-start(bf16[1,1024,3,5,128]{4,3,1,2,0:T(8,128)(2,1)S(1)} %copy.59) | copy-start | bytes 11796484
  5.0 31.4 %copy-start.5 = (f32[5,128]{1,0:T(8,128)S(1)}, f32[5,128]{1,0:T(8,128)}, u32[]{:S(2)}) copy-start(f32[5,128]{1,0:T(8,128)} %param.10) | copy-start | bytes 7684
  5.0 31.4 %copy-start.6 = (f32[5,128]{1,0:T(8,128)S(1)}, f32[5,128]{1,0:T(8,128)}, u32[]{:S(2)}) copy-start(f32[5,128]{1,0:T(8,128)} %param.11) | copy-start | bytes 7684
  44.1 30.6 %all-to-all-start.2 = ((bf16[5,1,1024,128]{3,0,1,2:T(8,128)(2,1)}), bf16[5,1,1024,128]{3,0,1,2:T(8,128)(2,1)}, u32[]{:S(2)}, u32[]{:S(2)}) async-start(bf16[5,1,1024,128]{3,0,1,2:T(8,128)(2,1)} %get-tuple-element.77), calls=%async_computation.2 | async-start | bytes 4194304 | tf_op jit(solution)/shard_map/all_to_all | solution.py:51
  57.2 22.5 %copy-start.2 = (bf16[5,1024,128]{2,1,0:T(8,128)(2,1)S(1)}, bf16[5,1024,128]{2,1,0:T(8,128)(2,1)}, u32[]{:S(2)}) copy-start(bf16[5,1024,128]{2,1,0:T(8,128)(2,1)} %custom-call) | copy-start | bytes 3932164
  74.7 42.7 %all-to-all-start.1 = ((bf16[5,1,1024,128]{3,0,1,2:T(8,128)(2,1)}), bf16[5,1,1024,128]{3,0,1,2:T(8,128)(2,1)}, u32[]{:S(2)}, u32[]{:S(2)}) async-start(bf16[5,1,1024,128]{3,0,1,2:T(8,128)(2,1)} %get-tuple-element.72), calls=%async_computation.1 | async-start | bytes 4194304 | tf_op jit(solution)/shard_map/all_to_all | solution.py:50
  115.2 2.3 %copy-start.3 = (bf16[5,1024,128]{2,1,0:T(8,128)(2,1)}, bf16[5,1024,128]{2,1,0:T(8,128)(2,1)S(1)}, u32[]{:S(2)}) copy-start(bf16[5,1024,128]{2,1,0:T(8,128)(2,1)S(1)} %get-tuple-element.37) | copy-start | bytes 3932164
  117.4 29.3 %all-to-all-start = ((bf16[5,1,1024,128]{3,0,1,2:T(8,128)(2,1)}), bf16[5,1,1024,128]{3,0,1,2:T(8,128)(2,1)S(1)}, u32[]{:S(2)}, u32[]{:S(2)}) async-start(bf16[5,1,1024,128]{3,0,1,2:T(8,128)(2,1)} %bitcast.74), calls=%async_computation | async-start | bytes 4194304 | tf_op jit(solution)/shard_map/all_to_all | solution.py:52
  150.3 7.0 %copy-start.8 = (s32[16]{0:T(128)S(1)}, s32[16]{0:T(128)}, u32[]{:S(2)}) copy-start(s32[16]{0:T(128)} %param.14) | copy-start | bytes 196
  151.7 20.0 %copy-start.4 = (bf16[5,1024,128]{2,1,0:T(8,128)(2,1)S(1)}, bf16[5,1024,128]{2,1,0:T(8,128)(2,1)}, u32[]{:S(2)}) copy-start(bf16[5,1024,128]{2,1,0:T(8,128)(2,1)} %copy-done.3) | copy-start | bytes 3932164
  151.7 20.0 %copy-start.7 = (f32[5,128]{1,0:T(8,128)S(1)}, f32[5,128]{1,0:T(8,128)}, u32[]{:S(2)}) copy-start(f32[5,128]{1,0:T(8,128)} %param.12) | copy-start | bytes 7684
  151.7 19.9 %all-to-all-start.3 = ((bf16[5,16,64,128]{3,2,0,1:T(8,128)(2,1)}), bf16[5,16,64,128]{3,2,0,1:T(8,128)(2,1)S(1)}, u32[]{:S(2)}, u32[]{:S(2)}) async-start(bf16[5,16,64,128]{3,2,0,1:T(8,128)(2,1)} %copy.31), calls=%async_computation.3 | async-start | bytes 2621440 | tf_op jit(solution)/shard_map/all_to_all | solution.py:72
where the time goes:
time: 209 us; the launch traced here: 206 us
  blocking collectives  57.2 us (27%)
  waiting for transfers between devices  41.5 us (20%)
  matrix products  30.5 us (15%)
  starting transfers between devices  23.9 us (11%)
  local copies, waits for them, and re-layouts  23.3 us (11%)
  other arithmetic  17.4 us (8%)
  loops' own time  9.45 us (5%)
  between operations  2.85 us (1%)
    unnamed x1, blocking collectives  33 us
    psum x1, blocking collectives, on_device(): query_total, key_total = lax.psum((query_sums, key_sums), 'space')  24.3 us
    all_to_all x1, waiting for transfers between devices, on_device(): lax.all_to_all(k_heads[:, None], 'tm', split_axis=2, concat_axis=1, tiled...  17.5 us
    all_to_all x1, waiting for transfers between devices, on_device(): lax.all_to_all(spatial_out[:, None], 'tm', split_axis=2, concat_axis=1, t...  14.2 us
    dot_general x5, matrix products, one_head(): jnp.dot(weights, value_head, preferred_element_type=jnp.float32)  10.9 us
    all_to_all x1, waiting for transfers between devices, on_device(): lax.all_to_all(temporal_mix, 'tm', split_axis=1, concat_axis=2, tiled=True)  9.84 us
    another operation x1, loops' own time, on_device(): lax.map(one_head, jnp.arange(q_heads.shape[0]))  9.45 us
    unnamed x21, local copies, waits for them, and re-layouts  8.9 us
  transfers between devices with their start and end apart: 4, of which 3 were waited for; matrix products, arithmetic and copies ran while one was open for 22% of the time, Pallas kernels for 0%

commit v1 on v0

v1 whole, which is shorter than its diff:
```python
import functools
import math

import jax
import jax.numpy as jnp
from jax import lax
from jax.experimental import pallas as pl
from jax.experimental.pallas import tpu as pltpu
from jax.sharding import PartitionSpec as P

HEADS = 40
HEAD = 128
PIXELS = 1024
FRAMES = 16
STEPS = 4
SPACE = 8
OWN_HEADS = HEADS // SPACE
BLOCK = PIXELS // FRAMES
ROWS = PIXELS // 128
QUERY_TILE = 256
GROUP = 8
GROUPS = BLOCK // GROUP
SIDE = 4

EPSILON = 1e-06
CHANNELS = HEADS * HEAD
SCALE_LOG2E = HEAD ** (-0.5) * math.log2(math.e)
MESH = pl.DeviceIdType.MESH


def offsets():
    def hops(o):
        return min(o[0], SIDE - o[0]) + min(o[1], SIDE - o[1])

    every = [(dy, dx) for dy in range(SIDE) for dx in range(SIDE) if (dy, dx) != (0, 0)]
    return sorted(every, key=lambda o: -hops(o))


def wait_bytes(ref, sem):
    pltpu.make_async_copy(ref, ref, sem).wait()


def column(row):
    return jnp.transpose(jnp.broadcast_to(row, (128, 128)))


def kernel(
    proj, q_gain, k_gain, head_weight, step_scale, timestep, frame_count,
    out,
    x, qk_in, o_out, o_in, ssq_out, ssq_in, fac_out, fac_in, normed, fcol, mix, scale, z, zpad,
    fin_out, fin_in, gains, weight, steps, live, steps_at, counts,
    local_sem, own_sem, qk_send, qk_recv, ssq_send, ssq_recv, fac_send, fac_recv,
    o_send, o_recv, fin_send, fin_recv, last_send,
):
    me = lax.axis_index("tm")
    sp = lax.axis_index("space")
    dp = lax.axis_index("dp")
    y, xx = me // SIDE, me % SIDE
    peers = [((y + dy) % SIDE) * SIDE + (xx + dx) % SIDE for dy, dx in offsets()]
    half = me % 2

    barrier = pltpu.get_barrier_semaphore()
    for t in peers:
        pl.semaphore_signal(barrier, inc=1, device_id=(t, sp, dp), device_id_type=MESH)
    for d in range(1, SPACE):
        pl.semaphore_signal(barrier, inc=1, device_id=(me, (sp + d) % SPACE, dp), device_id_type=MESH)

    loads = [
        pltpu.make_async_copy(proj.at[0], x.at[0], local_sem.at[0]),
        pltpu.make_async_copy(proj.at[1], x.at[1], local_sem.at[1]),
        pltpu.make_async_copy(proj.at[2], x.at[2], local_sem.at[2]),
        pltpu.make_async_copy(q_gain, gains.at[0], local_sem.at[3]),
        pltpu.make_async_copy(k_gain, gains.at[1], local_sem.at[4]),
        pltpu.make_async_copy(head_weight, weight, local_sem.at[5]),
        pltpu.make_async_copy(step_scale, steps, local_sem.at[6]),
        pltpu.make_async_copy(timestep, steps_at, local_sem.at[7]),
        pltpu.make_async_copy(frame_count, counts, local_sem.at[8]),
    ]
    for load in loads:
        load.start()

    pl.semaphore_wait(barrier, len(peers) + SPACE - 1)

    def rows_of(t):
        return pl.ds(pl.multiple_of(t * BLOCK, BLOCK), BLOCK)

    for t in peers:
        pltpu.make_async_remote_copy(
            proj.at[pl.ds(0, 2), :, rows_of(t)], qk_in.at[me], qk_send, qk_recv,
            device_id=(t, sp, dp), device_id_type=MESH,
        ).start()
    own = pltpu.make_async_copy(proj.at[pl.ds(0, 2), :, rows_of(me)], qk_in.at[me], own_sem)
    own.start()

    for c in range(2):
        loads[c].wait()
        for r in range(ROWS):
            total = jnp.zeros((128, 128), jnp.float32)
            for h in range(OWN_HEADS):
                part = x[c, h, 128 * r : 128 * (r + 1), :].astype(jnp.float32)
                total += part * part
            ssq_out[r, c : c + 1, :] = jnp.sum(jnp.transpose(total), axis=0, keepdims=True)
    for d in range(1, SPACE):
        pltpu.make_async_remote_copy(
            ssq_out, ssq_in.at[sp], ssq_send, ssq_recv,
            device_id=(me, (sp + d) % SPACE, dp), device_id_type=MESH,
        ).start()
    ssq_in[sp] = ssq_out[...]

    for load in loads[3:]:
        load.wait()
    lane = lax.broadcasted_iota(jnp.int32, (1, 128), 1)
    for b in range(GROUPS):
        row = jnp.zeros((1, 128), jnp.int32)
        for i in range(GROUP):
            row = jnp.where(lane % GROUP == i, counts[me * BLOCK + b * GROUP + i], row)
        live[b : b + 1, :] = row
    for f in range(FRAMES):
        scale[:, f : f + 1, :] = steps[:, pl.ds(steps_at[f], 1), :]
    z[...] = jnp.zeros_like(z)
    zpad[...] = jnp.zeros_like(zpad)

    wait_bytes(ssq_in.at[pl.ds(0, SPACE - 1)], ssq_recv)
    sums = ssq_in[0]
    for s in range(1, SPACE):
        sums += ssq_in[s]
    fac_out[...] = lax.rsqrt(sums / CHANNELS + EPSILON)
    for t in peers:
        pltpu.make_async_remote_copy(
            fac_out.at[t // 2], fac_in.at[me], fac_send, fac_recv,
            device_id=(t, sp, dp), device_id_type=MESH,
        ).start()
    fac_in[me] = fac_out[me // 2]

    for c in range(2):
        for r in range(ROWS):
            factor = column(fac_out[r, c : c + 1, :])
            for h in range(OWN_HEADS):
                rows = slice(128 * r, 128 * (r + 1))
                part = x[c, h, rows, :].astype(jnp.float32) * factor
                normed[c, h, rows, :] = (part * gains[c, h : h + 1, :]).astype(jnp.bfloat16)

    loads[2].wait()

    def spatial_head(h, carry):
        def tile(i, carry):
            rows = pl.ds(pl.multiple_of(i * QUERY_TILE, QUERY_TILE), QUERY_TILE)
            scores = lax.dot_general(
                normed[0, h, rows, :], normed[1, h], (((1,), (1,)), ((), ())),
                preferred_element_type=jnp.float32,
            )
            top = jnp.max(scores, axis=1, keepdims=True)
            exponent = jnp.exp2((scores - top) * SCALE_LOG2E)
            share = 1.0 / jnp.sum(exponent, axis=1, keepdims=True)
            weights = (exponent * share).astype(jnp.bfloat16)
            o_out[h, rows, :] = jnp.dot(
                weights, x[2, h], preferred_element_type=jnp.float32
            ).astype(jnp.bfloat16)
            return carry

        lax.fori_loop(0, PIXELS // QUERY_TILE, tile, 0)
        for t in peers:
            pltpu.make_async_remote_copy(
                o_out.at[h, rows_of(t)], o_in.at[h, me], o_send.at[h], o_recv.at[h],
                device_id=(t, sp, dp), device_id_type=MESH,
            ).start()
        o_in[h, me] = o_out[h, rows_of(me), :]
        return carry

    lax.fori_loop(0, OWN_HEADS, spatial_head, 0)

    wait_bytes(fac_in.at[pl.ds(0, FRAMES - 1)], fac_recv)
    for c in range(2):
        for f in range(FRAMES):
            fcol[c, f] = column(fac_in[f, c : c + 1, :])
    own.wait()
    wait_bytes(qk_in.at[pl.ds(0, FRAMES - 1)], qk_recv)
    side = FRAMES * GROUP
    at_row = lax.broadcasted_iota(jnp.int32, (side, side), 0)
    at_lane = lax.broadcasted_iota(jnp.int32, (side, side), 1)
    same = (at_row % GROUP) == (at_lane % GROUP)
    key_frame = at_lane // GROUP
    my_half = pl.ds(pl.multiple_of(half * BLOCK, BLOCK), BLOCK)

    def temporal_weights(h, carry):
        wide = []
        for c in range(2):
            part = qk_in[:, c, h].astype(jnp.float32) * fcol[c, :, my_half, :]
            wide.append(part * gains[c, pl.ds(h, 1), :].reshape(1, 1, HEAD))
        for b in range(GROUPS):
            queries, keys = (
                w[:, GROUP * b : GROUP * (b + 1), :].reshape(side, HEAD).astype(jnp.bfloat16)
                for w in wide
            )
            scores = lax.dot_general(
                queries, keys, (((1,), (1,)), ((), ())), preferred_element_type=jnp.float32
            )
            seen = same & (key_frame < live[b : b + 1, :])
            scores = jnp.where(seen, scores, -1e30)
            top = jnp.max(scores, axis=1, keepdims=True)
            exponent = jnp.exp2((scores - top) * SCALE_LOG2E)
            share = 1.0 / jnp.sum(exponent, axis=1, keepdims=True)
            mix[h, b] = (exponent * share).astype(jnp.bfloat16)
        return carry

    lax.fori_loop(0, OWN_HEADS, temporal_weights, 0)

    at_frame = lax.broadcasted_iota(jnp.int32, (FRAMES, GROUP, 128), 0)
    at_lane3 = lax.broadcasted_iota(jnp.int32, (FRAMES, GROUP, 128), 2)
    dot_lane = at_frame == at_lane3
    square_lane = at_frame + FRAMES == at_lane3

    def temporal_head(h, carry):
        wait_bytes(o_in.at[h, pl.ds(0, FRAMES - 1)], o_recv.at[h])
        spatial = o_in[h].astype(jnp.float32)
        row_scale = scale[h].reshape(FRAMES, 1, HEAD)
        row_weight = weight[pl.ds(h, 1), :].reshape(1, 1, HEAD)
        for b in range(GROUPS):
            pixels = slice(GROUP * b, GROUP * (b + 1))
            block = spatial[:, pixels, :]
            mixed = jnp.dot(
                mix[h, b], block.reshape(side, HEAD).astype(jnp.bfloat16),
                preferred_element_type=jnp.float32,
            ).astype(jnp.bfloat16).astype(jnp.float32)
            modulated = (block + mixed.reshape(FRAMES, GROUP, HEAD)) * row_scale
            dots = jnp.sum(modulated * row_weight, axis=2, keepdims=True)
            squares = jnp.sum(modulated * modulated, axis=2, keepdims=True)
            placed = jnp.where(dot_lane, dots, 0.0) + jnp.where(square_lane, squares, 0.0)
            z[pixels, :] += jnp.sum(placed, axis=0)
        return carry

    lax.fori_loop(0, OWN_HEADS, temporal_head, 0)

    zpad[my_half, :] = z[...]
    turned = jnp.transpose(zpad[...])
    for f in range(FRAMES):
        fin_out[f, 0:1, :] = turned[f : f + 1, :]
        fin_out[f, 1:2, :] = turned[FRAMES + f : FRAMES + f + 1, :]
    owner = me // 2
    slot = half * SPACE + sp
    for t in peers:
        pltpu.make_async_remote_copy(
            fin_out.at[t], fin_in.at[slot], fin_send, fin_recv,
            device_id=(t, owner, dp), device_id_type=MESH,
        ).start()

    @pl.when(sp == owner)
    def _():
        here = pltpu.make_async_copy(fin_out.at[me], fin_in.at[slot], fin_recv)
        here.start()

    @pl.when(sp != owner)
    def _():
        away = pltpu.make_async_remote_copy(
            fin_out.at[me], fin_in.at[slot], last_send, fin_recv,
            device_id=(me, owner, dp), device_id_type=MESH,
        )
        away.start()
        away.wait_send()

    wait_bytes(qk_in.at[pl.ds(0, FRAMES - 1)], qk_send)
    wait_bytes(ssq_in.at[pl.ds(0, SPACE - 1)], ssq_send)
    wait_bytes(fac_in.at[pl.ds(0, FRAMES - 1)], fac_send)
    for h in range(OWN_HEADS):
        wait_bytes(o_in.at[h, pl.ds(0, FRAMES - 1)], o_send.at[h])
    wait_bytes(fin_out.at[pl.ds(0, FRAMES - 1)], fin_send)
    wait_bytes(fin_in, fin_recv)
    totals = jnp.sum(fin_in[...], axis=0)
    out[...] = totals[0:1, :] * lax.rsqrt(totals[1:2, :] / CHANNELS + EPSILON)


def on_device(projected, q_gain, k_gain, head_weight, step_scale, timestep, frame_count):
    proj = jnp.transpose(projected[0], (1, 2, 0, 3))
    steps = jnp.transpose(step_scale, (1, 0, 2))
    any_space = pl.BlockSpec(memory_space=pl.ANY)
    bf16, f32 = jnp.bfloat16, jnp.float32
    dma = pltpu.SemaphoreType.DMA
    return pl.pallas_call(
        kernel,
        out_shape=jax.ShapeDtypeStruct((1, 128), f32),
        in_specs=[any_space] * 7,
        out_specs=pl.BlockSpec(memory_space=pltpu.VMEM),
        scratch_shapes=[
            pltpu.VMEM((3, OWN_HEADS, PIXELS, HEAD), bf16),
            pltpu.VMEM((FRAMES, 2, OWN_HEADS, BLOCK, HEAD), bf16),
            pltpu.VMEM((OWN_HEADS, PIXELS, HEAD), bf16),
            pltpu.VMEM((OWN_HEADS, FRAMES, BLOCK, HEAD), bf16),
            pltpu.VMEM((ROWS, 2, 128), f32),
            pltpu.VMEM((SPACE, ROWS, 2, 128), f32),
            pltpu.VMEM((ROWS, 2, 128), f32),
            pltpu.VMEM((FRAMES, 2, 128), f32),
            pltpu.VMEM((2, OWN_HEADS, PIXELS, HEAD), bf16),
            pltpu.VMEM((2, FRAMES, 128, 128), f32),
            pltpu.VMEM((OWN_HEADS, GROUPS, 128, 128), bf16),
            pltpu.VMEM((OWN_HEADS, FRAMES, HEAD), f32),
            pltpu.VMEM((BLOCK, 128), f32),
            pltpu.VMEM((128, 128), f32),
            pltpu.VMEM((FRAMES, 2, 128), f32),
            pltpu.VMEM((FRAMES, 2, 128), f32),
            pltpu.VMEM((2, OWN_HEADS, HEAD), f32),
            pltpu.VMEM((OWN_HEADS, HEAD), f32),
            pltpu.VMEM((OWN_HEADS, STEPS, HEAD), f32),
            pltpu.VMEM((GROUPS, 128), jnp.int32),
            pltpu.SMEM((FRAMES,), jnp.int32),
            pltpu.SMEM((PIXELS,), jnp.int32),
            dma((9,)), dma, dma, dma, dma, dma, dma, dma,
            dma((OWN_HEADS,)), dma((OWN_HEADS,)), dma, dma, dma,
        ],
        compiler_params=pltpu.CompilerParams(
            collective_id=0, has_side_effects=True, vmem_limit_bytes=56 * 2**20
        ),
        cost_estimate=pl.CostEstimate(
            flops=3_000_000_000, bytes_accessed=8_000_000, transcendentals=6_000_000
        ),
        name="space_time_attention",
    )(proj, q_gain, k_gain, head_weight, steps, timestep, frame_count)


def solution(mesh):
    in_specs = (
        P(("dp", "tm"), None, None, "space", None),
        P("space", None),
        P("space", None),
        P("space", None),
        P(None, "space", None),
        P("dp"),
        P("dp"),
    )
    out_specs = P(("dp", "tm"), "space")
    return jax.shard_map(
        on_device, mesh=mesh, in_specs=in_specs, out_specs=out_specs, check_vma=False
    )
```

time: 209 us -> 77.6 us (0.37); the launches traced: 206 us -> 77.5 us
  Pallas kernels: 0 us -> 76.3 us
  blocking collectives: 57.2 us -> 0 us
  waiting for transfers between devices: 41.5 us -> 0 us
  matrix products: 30.5 us -> 0 us
  starting transfers between devices: 23.9 us -> 0 us
  local copies, waits for them, and re-layouts: 23.3 us -> 1.19 us
  other arithmetic: 17.4 us -> 0 us
  loops' own time: 9.45 us -> 0 us
  between operations: 2.85 us -> 0.01 us
    pallas_call x0 -> x1, Pallas kernels: none -> 76.3 us  [on_device(): pl.pallas_call(kernel, out_shape=jax.ShapeDtypeStruct((1, 128), f32), in_...]
    all_to_all x4 -> x0, waiting for transfers between devices: 41.5 us -> none  [the longest x1 17.5 us: on_device(): lax.all_to_all(k_heads[:, None], 'tm', split_axis=2, concat_axis=1, tiled...]
    unnamed x1 -> x0, blocking collectives: 33 us -> none
    psum x1 -> x0, blocking collectives: 24.3 us -> none  [on_device(): query_total, key_total = lax.psum((query_sums, key_sums), 'space')]
    all_to_all x4 -> x0, starting transfers between devices: 23.9 us -> none  [the longest x1 6.75 us: on_device(): lax.all_to_all(k_heads[:, None], 'tm', split_axis=2, concat_axis=1, tiled...]
    dot_general x11 -> x0, matrix products: 22.9 us -> none  [the longest x5 10.9 us: one_head(): jnp.dot(weights, value_head, preferred_element_type=jnp.float32)]
    another operation x1 -> x0, loops' own time: 9.45 us -> none  [on_device(): lax.map(one_head, jnp.arange(q_heads.shape[0]))]
    reduce_sum x7 -> x0, other arithmetic: 9.05 us -> none  [the longest x1 4.47 us: on_device(): key_sums = jnp.sum(jnp.square(key_rows.astype(jnp.float32)), axis=(1, 2))]
  transfers between devices with their start and end apart: 4 -> 0, of which waited for: 3 -> 0; matrix products, arithmetic and copies ran while one was open for 22% -> 0% of each run, Pallas kernels for 0% -> 0%
where the time goes in v1:
time: 77.6 us; the launch traced here: 77.5 us
  Pallas kernels  76.3 us (98%)
  local copies, waits for them, and re-layouts  1.19 us (2%)
    pallas_call x1, Pallas kernels, on_device(): pl.pallas_call(kernel, out_shape=jax.ShapeDtypeStruct((1, 128), f32), in_...  76.3 us

profile of v1, /device:TPU:1, one launch (start us, length us, event | category | flops | bytes accessed | tf_op | source)
XLA Modules:
  0.0 77.5 jit_solution(10578191849786991295)
XLA Ops:
  0.0 76.3 %space_time_attention.1 = f32[1,128]{1,0:T(1,128)} custom-call(bf16[3,5,1024,128]{3,2,1,0:T(8,128)(2,1)} %bitcast.4, f32[5,128]{1,0:T(8,128)} %q_gain.1, f32[5,128]{1,0:T(8,128)} %k_gain.1, f32[5,128]{1,0:T(8,128)} %head_weight.1, f32[5,4,128]{2,1,0:T(4,128)} %bitcast.5, s32[16]{0:T(128)} %timestep.1, s32[1024]{0:T(1024)} %frame_count.1), custom_call_target="tpu_custom_call" | custom-call | flops 3000000000 | bytes 8000000 | tf_op jit(solution)/shard_map/space_time_attention/pallas_call | solution.py:278
  76.3 1.2 %copy.9 = f32[1,128]{1,0:T(1,128)} copy(f32[1,128]{1,0:T(1,128)} %space_time_attention.1) | data formatting | bytes 1024

commit v2 on v1

--- a/solution.py
+++ b/solution.py
@@ -20,6 +20,7 @@
 QUERY_TILE = 256
 GROUP = 8
 GROUPS = BLOCK // GROUP
+EARLY_HEADS = 3
 SIDE = 4
 
 EPSILON = 1e-06
@@ -28,12 +29,18 @@
 MESH = pl.DeviceIdType.MESH
 
 
-def offsets():
-    def hops(o):
-        return min(o[0], SIDE - o[0]) + min(o[1], SIDE - o[1])
-
-    every = [(dy, dx) for dy in range(SIDE) for dx in range(SIDE) if (dy, dx) != (0, 0)]
-    return sorted(every, key=lambda o: -hops(o))
+OFFSETS = (
+    (2, 2), (2, 3), (2, 1), (3, 2), (1, 2), (2, 0), (0, 2), (3, 1),
+    (1, 3), (3, 3), (1, 1), (3, 0), (1, 0), (0, 3), (0, 1),
+)
+
+
+def fold(i):
+    return i + i // 2 - 2 * (i // 3)
+
+
+def space_at(rank):
+    return 2 * fold(rank // 2) + rank % 2
 
 
 def wait_bytes(ref, sem):
@@ -47,23 +54,19 @@
 def kernel(
     proj, q_gain, k_gain, head_weight, step_scale, timestep, frame_count,
     out,
-    x, qk_in, o_out, o_in, ssq_out, ssq_in, fac_out, fac_in, normed, fcol, mix, scale, z, zpad,
+    x, qk_in, own_qk, o_out, o_in, ssq_out, ssq_in, fac_out, fac_in, normed, fcol, mix, scale, z,
     fin_out, fin_in, gains, weight, steps, live, steps_at, counts,
     local_sem, own_sem, qk_send, qk_recv, ssq_send, ssq_recv, fac_send, fac_recv,
-    o_send, o_recv, fin_send, fin_recv, last_send,
+    o_send, o_recv, fin_send, fin_recv, last_send, entered,
 ):
     me = lax.axis_index("tm")
     sp = lax.axis_index("space")
     dp = lax.axis_index("dp")
     y, xx = me // SIDE, me % SIDE
-    peers = [((y + dy) % SIDE) * SIDE + (xx + dx) % SIDE for dy, dx in offsets()]
+    down = [SIDE * jnp.where(y + d >= SIDE, y + d - SIDE, y + d) for d in range(SIDE)]
+    along = [jnp.where(xx + d >= SIDE, xx + d - SIDE, xx + d) for d in range(SIDE)]
+    peers = [down[dy] + along[dx] for dy, dx in OFFSETS]
     half = me % 2
-
-    barrier = pltpu.get_barrier_semaphore()
-    for t in peers:
-        pl.semaphore_signal(barrier, inc=1, device_id=(t, sp, dp), device_id_type=MESH)
-    for d in range(1, SPACE):
-        pl.semaphore_signal(barrier, inc=1, device_id=(me, (sp + d) % SPACE, dp), device_id_type=MESH)
 
     loads = [
         pltpu.make_async_copy(proj.at[0], x.at[0], local_sem.at[0]),
@@ -76,21 +79,51 @@
         pltpu.make_async_copy(timestep, steps_at, local_sem.at[7]),
         pltpu.make_async_copy(frame_count, counts, local_sem.at[8]),
     ]
-    for load in loads:
+    for load in loads[:2]:
         load.start()
 
-    pl.semaphore_wait(barrier, len(peers) + SPACE - 1)
+    barrier = pltpu.get_barrier_semaphore()
+    for t in peers:
+        pl.semaphore_signal(barrier, inc=1, device_id=(t, sp, dp), device_id_type=MESH)
+    rank = 2 * fold(sp // 2) + sp % 2
+
+    def announce(r, carry):
+        pl.semaphore_signal(
+            barrier, inc=1, device_id=(me, space_at(r), dp), device_id_type=MESH
+        )
+        return carry
+
+    lax.fori_loop(rank + 1, SPACE, announce, 0)
+
+    pl.semaphore_wait(barrier, len(peers) + rank)
+
+    def enter(r, carry):
+        pl.semaphore_signal(
+            entered, inc=1, device_id=(me, space_at(r), dp), device_id_type=MESH
+        )
+        return carry
+
+    def send_ssq(r, carry):
+        pltpu.make_async_remote_copy(
+            ssq_out, ssq_in.at[sp], ssq_send, ssq_recv,
+            device_id=(me, space_at(r), dp), device_id_type=MESH,
+        ).start()
+        return carry
 
     def rows_of(t):
         return pl.ds(pl.multiple_of(t * BLOCK, BLOCK), BLOCK)
 
-    for t in peers:
-        pltpu.make_async_remote_copy(
-            proj.at[pl.ds(0, 2), :, rows_of(t)], qk_in.at[me], qk_send, qk_recv,
-            device_id=(t, sp, dp), device_id_type=MESH,
-        ).start()
-    own = pltpu.make_async_copy(proj.at[pl.ds(0, 2), :, rows_of(me)], qk_in.at[me], own_sem)
-    own.start()
+    def send_qk(h):
+        for t in peers:
+            pltpu.make_async_remote_copy(
+                proj.at[pl.ds(0, 2), h, rows_of(t)], qk_in.at[h, me], qk_send.at[h], qk_recv.at[h],
+                device_id=(t, sp, dp), device_id_type=MESH,
+            ).start()
+
+    send_qk(0)
+    lax.fori_loop(0, rank, enter, 0)
+    for load in loads[2:]:
+        load.start()
 
     for c in range(2):
         loads[c].wait()
@@ -100,12 +133,28 @@
                 part = x[c, h, 128 * r : 128 * (r + 1), :].astype(jnp.float32)
                 total += part * part
             ssq_out[r, c : c + 1, :] = jnp.sum(jnp.transpose(total), axis=0, keepdims=True)
-    for d in range(1, SPACE):
-        pltpu.make_async_remote_copy(
-            ssq_out, ssq_in.at[sp], ssq_send, ssq_recv,
-            device_id=(me, (sp + d) % SPACE, dp), device_id_type=MESH,
-        ).start()
     ssq_in[sp] = ssq_out[...]
+    lax.fori_loop(0, rank, send_ssq, 0)
+
+    @pl.when(rank < SPACE // 2)
+    def _():
+        for h in range(1, EARLY_HEADS):
+            send_qk(h)
+
+    @pl.when(rank < SPACE - 1)
+    def _():
+        pl.semaphore_wait(entered, SPACE - 1 - rank)
+        lax.fori_loop(rank + 1, SPACE, send_ssq, 0)
+
+    @pl.when(rank >= SPACE // 2)
+    def _():
+        for h in range(1, EARLY_HEADS):
+            send_qk(h)
+
+    for h in range(EARLY_HEADS, OWN_HEADS - 1):
+        send_qk(h)
+    own = pltpu.make_async_copy(proj.at[pl.ds(0, 2), :, rows_of(me)], own_qk, own_sem)
+    own.start()
 
     for load in loads[3:]:
         load.wait()
@@ -118,7 +167,6 @@
     for f in range(FRAMES):
         scale[:, f : f + 1, :] = steps[:, pl.ds(steps_at[f], 1), :]
     z[...] = jnp.zeros_like(z)
-    zpad[...] = jnp.zeros_like(zpad)
 
     wait_bytes(ssq_in.at[pl.ds(0, SPACE - 1)], ssq_recv)
     sums = ssq_in[0]
@@ -130,6 +178,7 @@
             fac_out.at[t // 2], fac_in.at[me], fac_send, fac_recv,
             device_id=(t, sp, dp), device_id_type=MESH,
         ).start()
+    send_qk(OWN_HEADS - 1)
     fac_in[me] = fac_out[me // 2]
 
     for c in range(2):
@@ -174,7 +223,9 @@
         for f in range(FRAMES):
             fcol[c, f] = column(fac_in[f, c : c + 1, :])
     own.wait()
-    wait_bytes(qk_in.at[pl.ds(0, FRAMES - 1)], qk_recv)
+    for c in range(2):
+        for h in range(OWN_HEADS):
+            qk_in[h, me, c] = own_qk[c, h]
     side = FRAMES * GROUP
     at_row = lax.broadcasted_iota(jnp.int32, (side, side), 0)
     at_lane = lax.broadcasted_iota(jnp.int32, (side, side), 1)
@@ -183,9 +234,10 @@
     my_half = pl.ds(pl.multiple_of(half * BLOCK, BLOCK), BLOCK)
 
     def temporal_weights(h, carry):
+        wait_bytes(qk_in.at[h, pl.ds(0, FRAMES - 1)], qk_recv.at[h])
         wide = []
         for c in range(2):
-            part = qk_in[:, c, h].astype(jnp.float32) * fcol[c, :, my_half, :]
+            part = qk_in[h, :, c].astype(jnp.float32) * fcol[c, :, my_half, :]
             wide.append(part * gains[c, pl.ds(h, 1), :].reshape(1, 1, HEAD))
         for b in range(GROUPS):
             queries, keys = (
@@ -226,13 +278,13 @@
             dots = jnp.sum(modulated * row_weight, axis=2, keepdims=True)
             squares = jnp.sum(modulated * modulated, axis=2, keepdims=True)
             placed = jnp.where(dot_lane, dots, 0.0) + jnp.where(square_lane, squares, 0.0)
-            z[pixels, :] += jnp.sum(placed, axis=0)
+            at = pl.ds(pl.multiple_of(half * BLOCK + GROUP * b, GROUP), GROUP)
+            z[at, :] += jnp.sum(placed, axis=0)
         return carry
 
     lax.fori_loop(0, OWN_HEADS, temporal_head, 0)
 
-    zpad[my_half, :] = z[...]
-    turned = jnp.transpose(zpad[...])
+    turned = jnp.transpose(z[...])
     for f in range(FRAMES):
         fin_out[f, 0:1, :] = turned[f : f + 1, :]
         fin_out[f, 1:2, :] = turned[FRAMES + f : FRAMES + f + 1, :]
@@ -258,10 +310,10 @@
         away.start()
         away.wait_send()
 
-    wait_bytes(qk_in.at[pl.ds(0, FRAMES - 1)], qk_send)
     wait_bytes(ssq_in.at[pl.ds(0, SPACE - 1)], ssq_send)
     wait_bytes(fac_in.at[pl.ds(0, FRAMES - 1)], fac_send)
     for h in range(OWN_HEADS):
+        wait_bytes(qk_in.at[h, pl.ds(0, FRAMES - 1)], qk_send.at[h])
         wait_bytes(o_in.at[h, pl.ds(0, FRAMES - 1)], o_send.at[h])
     wait_bytes(fin_out.at[pl.ds(0, FRAMES - 1)], fin_send)
     wait_bytes(fin_in, fin_recv)
@@ -282,7 +334,8 @@
         out_specs=pl.BlockSpec(memory_space=pltpu.VMEM),
         scratch_shapes=[
             pltpu.VMEM((3, OWN_HEADS, PIXELS, HEAD), bf16),
-            pltpu.VMEM((FRAMES, 2, OWN_HEADS, BLOCK, HEAD), bf16),
+            pltpu.VMEM((OWN_HEADS, FRAMES, 2, BLOCK, HEAD), bf16),
+            pltpu.VMEM((2, OWN_HEADS, BLOCK, HEAD), bf16),
             pltpu.VMEM((OWN_HEADS, PIXELS, HEAD), bf16),
             pltpu.VMEM((OWN_HEADS, FRAMES, BLOCK, HEAD), bf16),
             pltpu.VMEM((ROWS, 2, 128), f32),
@@ -293,7 +346,6 @@
             pltpu.VMEM((2, FRAMES, 128, 128), f32),
             pltpu.VMEM((OWN_HEADS, GROUPS, 128, 128), bf16),
             pltpu.VMEM((OWN_HEADS, FRAMES, HEAD), f32),
-            pltpu.VMEM((BLOCK, 128), f32),
             pltpu.VMEM((128, 128), f32),
             pltpu.VMEM((FRAMES, 2, 128), f32),
             pltpu.VMEM((FRAMES, 2, 128), f32),
@@ -303,8 +355,9 @@
             pltpu.VMEM((GROUPS, 128), jnp.int32),
             pltpu.SMEM((FRAMES,), jnp.int32),
             pltpu.SMEM((PIXELS,), jnp.int32),
-            dma((9,)), dma, dma, dma, dma, dma, dma, dma,
+            dma((9,)), dma, dma((OWN_HEADS,)), dma((OWN_HEADS,)), dma, dma, dma, dma,
             dma((OWN_HEADS,)), dma((OWN_HEADS,)), dma, dma, dma,
+            pltpu.SemaphoreType.REGULAR,
         ],
         compiler_params=pltpu.CompilerParams(
             collective_id=0, has_side_effects=True, vmem_limit_bytes=56 * 2**20

time: 77.6 us -> 71.7 us (0.924)
  Pallas kernels: 76.3 us -> 70.4 us
    pallas_call x1, Pallas kernels: 76.3 us -> 70.4 us  [on_device(): pl.pallas_call(kernel, out_shape=jax.ShapeDtypeStruct((1, 128), f32), in_...]
where the time goes in v2:
time: 71.7 us; the launch traced here: 71.6 us
  Pallas kernels  70.4 us (98%)
  local copies, waits for them, and re-layouts  1.19 us (2%)
    pallas_call x1, Pallas kernels, on_device(): pl.pallas_call(kernel, out_shape=jax.ShapeDtypeStruct((1, 128), f32), in_...  70.4 us

profile of v2, /device:TPU:1, one launch (start us, length us, event | category | flops | bytes accessed | tf_op | source)
XLA Modules:
  0.0 71.6 jit_solution(13539016837968209992)
XLA Ops:
  0.0 70.4 %space_time_attention.1 = f32[1,128]{1,0:T(1,128)} custom-call(bf16[3,5,1024,128]{3,2,1,0:T(8,128)(2,1)} %bitcast.4, f32[5,128]{1,0:T(8,128)} %q_gain.1, f32[5,128]{1,0:T(8,128)} %k_gain.1, f32[5,128]{1,0:T(8,128)} %head_weight.1, f32[5,4,128]{2,1,0:T(4,128)} %bitcast.5, s32[16]{0:T(128)} %timestep.1, s32[1024]{0:T(1024)} %frame_count.1), custom_call_target="tpu_custom_call" | custom-call | flops 3000000000 | bytes 8000000 | tf_op jit(solution)/shard_map/space_time_attention/pallas_call | solution.py:330
  70.4 1.2 %copy.9 = f32[1,128]{1,0:T(1,128)} copy(f32[1,128]{1,0:T(1,128)} %space_time_attention.1) | data formatting | bytes 1024

commit v3 on v2

--- a/solution.py
+++ b/solution.py
@@ -22,6 +22,8 @@
 GROUPS = BLOCK // GROUP
 EARLY_HEADS = 3
 SIDE = 4
+GUEST = OWN_HEADS
+PART = 16
 
 EPSILON = 1e-06
 CHANNELS = HEADS * HEAD
@@ -55,17 +57,17 @@
     proj, q_gain, k_gain, head_weight, step_scale, timestep, frame_count,
     out,
     x, qk_in, own_qk, o_out, o_in, ssq_out, ssq_in, fac_out, fac_in, normed, fcol, mix, scale, z,
-    fin_out, fin_in, gains, weight, steps, live, steps_at, counts,
+    fin_out, fin_in, gains, weight, steps, head_out, head_in, live, steps_at, counts,
     local_sem, own_sem, qk_send, qk_recv, ssq_send, ssq_recv, fac_send, fac_recv,
-    o_send, o_recv, fin_send, fin_recv, last_send, entered,
+    o_send, o_recv, fin_send, fin_recv, last_send, entered, guest_send, head_recv,
 ):
     me = lax.axis_index("tm")
     sp = lax.axis_index("space")
     dp = lax.axis_index("dp")
     y, xx = me // SIDE, me % SIDE
-    down = [SIDE * jnp.where(y + d >= SIDE, y + d - SIDE, y + d) for d in range(SIDE)]
+    down = [jnp.where(y + d >= SIDE, y + d - SIDE, y + d) for d in range(SIDE)]
     along = [jnp.where(xx + d >= SIDE, xx + d - SIDE, xx + d) for d in range(SIDE)]
-    peers = [down[dy] + along[dx] for dy, dx in OFFSETS]
+    peers = [SIDE * down[dy] + along[dx] for dy, dx in OFFSETS]
     half = me % 2
 
     loads = [
@@ -87,6 +89,21 @@
         pl.semaphore_signal(barrier, inc=1, device_id=(t, sp, dp), device_id_type=MESH)
     rank = 2 * fold(sp // 2) + sp % 2
 
+    late = sp >= SPACE // 2
+    partner = 2 * (SPACE // 2 - 1 - sp // 2) + sp % 2
+    kinds = [[v + u - jnp.where(v + u >= SIDE, SIDE, 0) for u in along] for v in down]
+    kind_of = [kinds[dy][dx] for dy, dx in OFFSETS]
+    given = kinds[0][0]
+
+    @pl.when(jnp.logical_not(late))
+    def _():
+        for t in peers:
+            pl.semaphore_signal(
+                barrier, inc=1, device_id=(t, partner, dp), device_id_type=MESH
+            )
+
+    held = len(peers) + rank + jnp.where(late, len(peers), 0)
+
     def announce(r, carry):
         pl.semaphore_signal(
             barrier, inc=1, device_id=(me, space_at(r), dp), device_id_type=MESH
@@ -95,7 +112,7 @@
 
     lax.fori_loop(rank + 1, SPACE, announce, 0)
 
-    pl.semaphore_wait(barrier, len(peers) + rank)
+    pl.semaphore_wait(barrier, held)
 
     def enter(r, carry):
         pl.semaphore_signal(
@@ -113,12 +130,64 @@
     def rows_of(t):
         return pl.ds(pl.multiple_of(t * BLOCK, BLOCK), BLOCK)
 
+    def push(source, target, slot, start, size, to, send, recv):
+        pltpu.make_async_remote_copy(
+            source(start, size), target(slot, start, size), send, recv.at[slot],
+            device_id=to, device_id_type=MESH,
+        ).start()
+
+    def block_source(ref, h):
+        def at(t):
+            def rows(start, size):
+                first = pl.multiple_of(t * BLOCK + start, PART)
+                return ref(h, pl.ds(first, size))
+
+            return rows
+
+        return at
+
+    def qk_target(slot, start, size):
+        return qk_in.at[slot, me, :, pl.ds(start, size)]
+
+    def o_target(slot, start, size):
+        return o_in.at[slot, me, pl.ds(start, size)]
+
+    def push_main(source, target, h, send, recv):
+        for t, kind in zip(peers, kind_of):
+            moves = jnp.logical_and(late, kind == h)
+
+            @pl.when(jnp.logical_not(moves))
+            def _():
+                push(source(t), target, h, 0, BLOCK, (t, sp, dp), send.at[h], recv)
+
+            @pl.when(moves)
+            def _():
+                push(source(t), target, h, PART, BLOCK - PART, (t, sp, dp), send.at[h], recv)
+
+    def push_moved(source, target, h, send, recv, own_send):
+        @pl.when(late)
+        def _():
+            for t, kind in zip(peers, kind_of):
+
+                @pl.when(kind == h)
+                def _():
+                    push(source(t), target, GUEST, 0, PART, (t, partner, dp), send.at[h], recv)
+
+            @pl.when(given == h)
+            def _():
+                push(source(me), target, GUEST, 0, PART, (me, partner, dp), own_send, recv)
+
+    def qk_source(h):
+        return block_source(lambda h, rows: proj.at[pl.ds(0, 2), h, rows], h)
+
+    def o_source(h):
+        return block_source(lambda h, rows: o_out.at[h, rows], h)
+
     def send_qk(h):
-        for t in peers:
-            pltpu.make_async_remote_copy(
-                proj.at[pl.ds(0, 2), h, rows_of(t)], qk_in.at[h, me], qk_send.at[h], qk_recv.at[h],
-                device_id=(t, sp, dp), device_id_type=MESH,
-            ).start()
+        push_main(qk_source(h), qk_target, h, qk_send, qk_recv)
+
+    def send_moved_qk(h):
+        push_moved(qk_source(h), qk_target, h, qk_send, qk_recv, guest_send.at[0])
 
     send_qk(0)
     lax.fori_loop(0, rank, enter, 0)
@@ -148,11 +217,14 @@
 
     @pl.when(rank >= SPACE // 2)
     def _():
+        send_moved_qk(0)
         for h in range(1, EARLY_HEADS):
             send_qk(h)
+            send_moved_qk(h)
 
     for h in range(EARLY_HEADS, OWN_HEADS - 1):
         send_qk(h)
+        send_moved_qk(h)
     own = pltpu.make_async_copy(proj.at[pl.ds(0, 2), :, rows_of(me)], own_qk, own_sem)
     own.start()
 
@@ -165,7 +237,20 @@
             row = jnp.where(lane % GROUP == i, counts[me * BLOCK + b * GROUP + i], row)
         live[b : b + 1, :] = row
     for f in range(FRAMES):
-        scale[:, f : f + 1, :] = steps[:, pl.ds(steps_at[f], 1), :]
+        scale[pl.ds(0, OWN_HEADS), f : f + 1, :] = steps[:, pl.ds(steps_at[f], 1), :]
+
+    @pl.when(late)
+    def _():
+        for c in range(2):
+            head_out[c : c + 1, :] = gains[c, pl.ds(given, 1), :]
+        for row in range(2, 4):
+            head_out[row : row + 1, :] = weight[pl.ds(given, 1), :]
+        head_out[4:8, :] = steps[given]
+        pltpu.make_async_remote_copy(
+            head_out, head_in, guest_send.at[1], head_recv,
+            device_id=(me, partner, dp), device_id_type=MESH,
+        ).start()
+
     z[...] = jnp.zeros_like(z)
 
     wait_bytes(ssq_in.at[pl.ds(0, SPACE - 1)], ssq_recv)
@@ -208,11 +293,8 @@
             return carry
 
         lax.fori_loop(0, PIXELS // QUERY_TILE, tile, 0)
-        for t in peers:
-            pltpu.make_async_remote_copy(
-                o_out.at[h, rows_of(t)], o_in.at[h, me], o_send.at[h], o_recv.at[h],
-                device_id=(t, sp, dp), device_id_type=MESH,
-            ).start()
+        push_main(o_source(h), o_target, h, o_send, o_recv)
+        push_moved(o_source(h), o_target, h, o_send, o_recv, guest_send.at[2])
         o_in[h, me] = o_out[h, rows_of(me), :]
         return carry
 
@@ -226,6 +308,18 @@
     for c in range(2):
         for h in range(OWN_HEADS):
             qk_in[h, me, c] = own_qk[c, h]
+
+    @pl.when(late)
+    def _():
+        qk_in[given, :, :, 0:PART, :] = jnp.zeros((FRAMES, 2, PART, HEAD), jnp.bfloat16)
+        o_in[given, :, 0:PART, :] = jnp.zeros((FRAMES, PART, HEAD), jnp.bfloat16)
+
+    @pl.when(jnp.logical_not(late))
+    def _():
+        rest = BLOCK - PART
+        qk_in[GUEST, :, :, PART:BLOCK, :] = jnp.zeros((FRAMES, 2, rest, HEAD), jnp.bfloat16)
+        o_in[GUEST, :, PART:BLOCK, :] = jnp.zeros((FRAMES, rest, HEAD), jnp.bfloat16)
+
     side = FRAMES * GROUP
     at_row = lax.broadcasted_iota(jnp.int32, (side, side), 0)
     at_lane = lax.broadcasted_iota(jnp.int32, (side, side), 1)
@@ -233,12 +327,45 @@
     key_frame = at_lane // GROUP
     my_half = pl.ds(pl.multiple_of(half * BLOCK, BLOCK), BLOCK)
 
+    heads = OWN_HEADS + jnp.where(late, 0, 1)
+
+    @pl.when(jnp.logical_not(late))
+    def _():
+        wait_bytes(head_in, head_recv)
+        for f in range(FRAMES):
+            scale[GUEST, f : f + 1, :] = head_in[pl.ds(4 + steps_at[f], 1), :]
+
+    def arrive(part, sems, h):
+        less = jnp.logical_and(late, given == h)
+
+        @pl.when(jnp.logical_and(h < GUEST, jnp.logical_not(less)))
+        def _():
+            wait_bytes(part(h, FRAMES - 1, BLOCK), sems.at[h])
+
+        @pl.when(less)
+        def _():
+            wait_bytes(part(h, FRAMES - 1, BLOCK - PART), sems.at[h])
+
+        @pl.when(h == GUEST)
+        def _():
+            wait_bytes(part(h, FRAMES, PART), sems.at[h])
+
+    def qk_part(h, frames, rows):
+        return qk_in.at[h, pl.ds(0, frames), :, pl.ds(0, rows)]
+
+    def o_part(h, frames, rows):
+        return o_in.at[h, pl.ds(0, frames), pl.ds(0, rows)]
+
+    def of_head(own, row, h):
+        return jnp.where(h < GUEST, own[pl.ds(jnp.minimum(h, GUEST - 1), 1), :], row)
+
     def temporal_weights(h, carry):
-        wait_bytes(qk_in.at[h, pl.ds(0, FRAMES - 1)], qk_recv.at[h])
+        arrive(qk_part, qk_recv, h)
         wide = []
         for c in range(2):
             part = qk_in[h, :, c].astype(jnp.float32) * fcol[c, :, my_half, :]
-            wide.append(part * gains[c, pl.ds(h, 1), :].reshape(1, 1, HEAD))
+            gain = of_head(gains.at[c], head_in[c : c + 1, :], h)
+            wide.append(part * gain.reshape(1, 1, HEAD))
         for b in range(GROUPS):
             queries, keys = (
                 w[:, GROUP * b : GROUP * (b + 1), :].reshape(side, HEAD).astype(jnp.bfloat16)
@@ -255,7 +382,7 @@
             mix[h, b] = (exponent * share).astype(jnp.bfloat16)
         return carry
 
-    lax.fori_loop(0, OWN_HEADS, temporal_weights, 0)
+    lax.fori_loop(0, heads, temporal_weights, 0)
 
     at_frame = lax.broadcasted_iota(jnp.int32, (FRAMES, GROUP, 128), 0)
     at_lane3 = lax.broadcasted_iota(jnp.int32, (FRAMES, GROUP, 128), 2)
@@ -263,10 +390,10 @@
     square_lane = at_frame + FRAMES == at_lane3
 
     def temporal_head(h, carry):
-        wait_bytes(o_in.at[h, pl.ds(0, FRAMES - 1)], o_recv.at[h])
+        arrive(o_part, o_recv, h)
         spatial = o_in[h].astype(jnp.float32)
         row_scale = scale[h].reshape(FRAMES, 1, HEAD)
-        row_weight = weight[pl.ds(h, 1), :].reshape(1, 1, HEAD)
+        row_weight = of_head(weight, head_in[2:3, :], h).reshape(1, 1, HEAD)
         for b in range(GROUPS):
             pixels = slice(GROUP * b, GROUP * (b + 1))
             block = spatial[:, pixels, :]
@@ -282,7 +409,7 @@
             z[at, :] += jnp.sum(placed, axis=0)
         return carry
 
-    lax.fori_loop(0, OWN_HEADS, temporal_head, 0)
+    lax.fori_loop(0, heads, temporal_head, 0)
 
     turned = jnp.transpose(z[...])
     for f in range(FRAMES):
@@ -315,10 +442,16 @@
     for h in range(OWN_HEADS):
         wait_bytes(qk_in.at[h, pl.ds(0, FRAMES - 1)], qk_send.at[h])
         wait_bytes(o_in.at[h, pl.ds(0, FRAMES - 1)], o_send.at[h])
+
+    @pl.when(late)
+    def _():
+        wait_bytes(qk_part(GUEST, 1, PART), guest_send.at[0])
+        wait_bytes(head_out, guest_send.at[1])
+        wait_bytes(o_part(GUEST, 1, PART), guest_send.at[2])
+
     wait_bytes(fin_out.at[pl.ds(0, FRAMES - 1)], fin_send)
     wait_bytes(fin_in, fin_recv)
-    totals = jnp.sum(fin_in[...], axis=0)
-    out[...] = totals[0:1, :] * lax.rsqrt(totals[1:2, :] / CHANNELS + EPSILON)
+    out[...] = jnp.sum(fin_in[...], axis=0)
 
 
 def on_device(projected, q_gain, k_gain, head_weight, step_scale, timestep, frame_count):
@@ -327,37 +460,39 @@
     any_space = pl.BlockSpec(memory_space=pl.ANY)
     bf16, f32 = jnp.bfloat16, jnp.float32
     dma = pltpu.SemaphoreType.DMA
-    return pl.pallas_call(
+    totals = pl.pallas_call(
         kernel,
-        out_shape=jax.ShapeDtypeStruct((1, 128), f32),
+        out_shape=jax.ShapeDtypeStruct((2, 128), f32),
         in_specs=[any_space] * 7,
         out_specs=pl.BlockSpec(memory_space=pltpu.VMEM),
         scratch_shapes=[
             pltpu.VMEM((3, OWN_HEADS, PIXELS, HEAD), bf16),
-            pltpu.VMEM((OWN_HEADS, FRAMES, 2, BLOCK, HEAD), bf16),
+            pltpu.VMEM((OWN_HEADS + 1, FRAMES, 2, BLOCK, HEAD), bf16),
             pltpu.VMEM((2, OWN_HEADS, BLOCK, HEAD), bf16),
             pltpu.VMEM((OWN_HEADS, PIXELS, HEAD), bf16),
-            pltpu.VMEM((OWN_HEADS, FRAMES, BLOCK, HEAD), bf16),
+            pltpu.VMEM((OWN_HEADS + 1, FRAMES, BLOCK, HEAD), bf16),
             pltpu.VMEM((ROWS, 2, 128), f32),
             pltpu.VMEM((SPACE, ROWS, 2, 128), f32),
             pltpu.VMEM((ROWS, 2, 128), f32),
             pltpu.VMEM((FRAMES, 2, 128), f32),
             pltpu.VMEM((2, OWN_HEADS, PIXELS, HEAD), bf16),
             pltpu.VMEM((2, FRAMES, 128, 128), f32),
-            pltpu.VMEM((OWN_HEADS, GROUPS, 128, 128), bf16),
-            pltpu.VMEM((OWN_HEADS, FRAMES, HEAD), f32),
+            pltpu.VMEM((OWN_HEADS + 1, GROUPS, 128, 128), bf16),
+            pltpu.VMEM((OWN_HEADS + 1, FRAMES, HEAD), f32),
             pltpu.VMEM((128, 128), f32),
             pltpu.VMEM((FRAMES, 2, 128), f32),
             pltpu.VMEM((FRAMES, 2, 128), f32),
             pltpu.VMEM((2, OWN_HEADS, HEAD), f32),
             pltpu.VMEM((OWN_HEADS, HEAD), f32),
             pltpu.VMEM((OWN_HEADS, STEPS, HEAD), f32),
+            pltpu.VMEM((8, HEAD), f32),
+            pltpu.VMEM((8, HEAD), f32),
             pltpu.VMEM((GROUPS, 128), jnp.int32),
             pltpu.SMEM((FRAMES,), jnp.int32),
             pltpu.SMEM((PIXELS,), jnp.int32),
-            dma((9,)), dma, dma((OWN_HEADS,)), dma((OWN_HEADS,)), dma, dma, dma, dma,
-            dma((OWN_HEADS,)), dma((OWN_HEADS,)), dma, dma, dma,
-            pltpu.SemaphoreType.REGULAR,
+            dma((9,)), dma, dma((OWN_HEADS,)), dma((OWN_HEADS + 1,)), dma, dma, dma, dma,
+            dma((OWN_HEADS,)), dma((OWN_HEADS + 1,)), dma, dma, dma,
+            pltpu.SemaphoreType.REGULAR, dma((3,)), dma,
         ],
         compiler_params=pltpu.CompilerParams(
             collective_id=0, has_side_effects=True, vmem_limit_bytes=56 * 2**20
@@ -367,6 +502,7 @@
         ),
         name="space_time_attention",
     )(proj, q_gain, k_gain, head_weight, steps, timestep, frame_count)
+    return totals[0:1] * lax.rsqrt(totals[1:2] / CHANNELS + EPSILON)
 
 
 def solution(mesh):

time: 71.7 us -> 69.8 us (0.974)
  Pallas kernels: 70.4 us -> 68.4 us
  other arithmetic: 0 us -> 1.28 us
  local copies, waits for them, and re-layouts: 1.19 us -> 0 us
    pallas_call x1, Pallas kernels: 70.4 us -> 68.4 us  [on_device(): pl.pallas_call(kernel, out_shape=jax.ShapeDtypeStruct((2, 128), f32), in_...]
    mul x0 -> x1, other arithmetic: none -> 1.28 us  [on_device(): return totals[0:1] * lax.rsqrt(totals[1:2] / CHANNELS + EPSILON)]
    unnamed x1 -> x0, local copies, waits for them, and re-layouts: 1.19 us -> none
where the time goes in v3:
time: 69.8 us; the launch traced here: 69.6 us
  Pallas kernels  68.4 us (98%)
  other arithmetic  1.28 us (2%)
    pallas_call x1, Pallas kernels, on_device(): pl.pallas_call(kernel, out_shape=jax.ShapeDtypeStruct((2, 128), f32), in_...  68.4 us

profile of v3, /device:TPU:1, one launch (start us, length us, event | category | flops | bytes accessed | tf_op | source)
XLA Modules:
  0.0 69.6 jit_solution(9837538107106597028)
XLA Ops:
  0.0 68.4 %space_time_attention.1 = f32[2,128]{1,0:T(2,128)} custom-call(bf16[3,5,1024,128]{3,2,1,0:T(8,128)(2,1)} %bitcast.4, f32[5,128]{1,0:T(8,128)} %q_gain.1, f32[5,128]{1,0:T(8,128)} %k_gain.1, f32[5,128]{1,0:T(8,128)} %head_weight.1, f32[5,4,128]{2,1,0:T(4,128)} %bitcast.5, s32[16]{0:T(128)} %timestep.1, s32[1024]{0:T(1024)} %frame_count.1), custom_call_target="tpu_custom_call" | custom-call | flops 3000000000 | bytes 8000000 | tf_op jit(solution)/shard_map/space_time_attention/pallas_call | solution.py:463
  68.4 1.3 %rsqrt_multiply_fusion = f32[1,128]{1,0:T(1,128)} fusion(f32[2,128]{1,0:T(2,128)} %space_time_attention.1), kind=kLoop, calls=%fused_computation | loop fusion | flops 384 | bytes 1536 | tf_op jit(solution)/shard_map/mul | solution.py:505

commit v4 on v3

--- a/solution.py
+++ b/solution.py
@@ -23,6 +23,7 @@
 EARLY_HEADS = 3
 SIDE = 4
 GUEST = OWN_HEADS
+SLOTS = OWN_HEADS + 2
 PART = 16
 
 EPSILON = 1e-06
@@ -35,14 +36,6 @@
     (2, 2), (2, 3), (2, 1), (3, 2), (1, 2), (2, 0), (0, 2), (3, 1),
     (1, 3), (3, 3), (1, 1), (3, 0), (1, 0), (0, 3), (0, 1),
 )
-
-
-def fold(i):
-    return i + i // 2 - 2 * (i // 3)
-
-
-def space_at(rank):
-    return 2 * fold(rank // 2) + rank % 2
 
 
 def wait_bytes(ref, sem):
@@ -59,7 +52,7 @@
     x, qk_in, own_qk, o_out, o_in, ssq_out, ssq_in, fac_out, fac_in, normed, fcol, mix, scale, z,
     fin_out, fin_in, gains, weight, steps, head_out, head_in, live, steps_at, counts,
     local_sem, own_sem, qk_send, qk_recv, ssq_send, ssq_recv, fac_send, fac_recv,
-    o_send, o_recv, fin_send, fin_recv, last_send, entered, guest_send, head_recv,
+    o_send, o_recv, fin_send, fin_recv, last_send, entered, guest_qk_send, guest_o_send, head_send, head_recv,
 ):
     me = lax.axis_index("tm")
     sp = lax.axis_index("space")
@@ -87,26 +80,45 @@
     barrier = pltpu.get_barrier_semaphore()
     for t in peers:
         pl.semaphore_signal(barrier, inc=1, device_id=(t, sp, dp), device_id_type=MESH)
-    rank = 2 * fold(sp // 2) + sp % 2
-
-    late = sp >= SPACE // 2
-    partner = 2 * (SPACE // 2 - 1 - sp // 2) + sp % 2
+    rank = sp
+
     kinds = [[v + u - jnp.where(v + u >= SIDE, SIDE, 0) for u in along] for v in down]
     kind_of = [kinds[dy][dx] for dy, dx in OFFSETS]
-    given = kinds[0][0]
-
-    @pl.when(jnp.logical_not(late))
+    kind = kinds[0][0]
+    late = sp >= SPACE // 2
+    last = jnp.logical_and(late, sp < SPACE // 2 + 2)
+    partner = 2 * (SPACE // 2 - 1 - sp // 2) + sp % 2
+
+    def next_head(k):
+        return k + 1 - jnp.where(k == SIDE - 1, SIDE, 0)
+
+    gifts = (
+        (late, partner, lambda k: k, lambda k: k >= 0, GUEST),
+        (last, sp % 2, next_head, lambda k: k % 2 == 0, GUEST + 1),
+    )
+    first_host = jnp.logical_not(late)
+    second_host = jnp.logical_and(sp < 2, kind % 2 == 0)
+
+    @pl.when(first_host)
     def _():
         for t in peers:
             pl.semaphore_signal(
                 barrier, inc=1, device_id=(t, partner, dp), device_id_type=MESH
             )
 
+    @pl.when(second_host)
+    def _():
+        for t in peers:
+            pl.semaphore_signal(
+                barrier, inc=1, device_id=(t, sp + SPACE // 2, dp), device_id_type=MESH
+            )
+
     held = len(peers) + rank + jnp.where(late, len(peers), 0)
+    held += jnp.where(last, FRAMES // 2 - jnp.where(kind % 2 == 0, 1, 0), 0)
 
     def announce(r, carry):
         pl.semaphore_signal(
-            barrier, inc=1, device_id=(me, space_at(r), dp), device_id_type=MESH
+            barrier, inc=1, device_id=(me, r, dp), device_id_type=MESH
         )
         return carry
 
@@ -116,14 +128,14 @@
 
     def enter(r, carry):
         pl.semaphore_signal(
-            entered, inc=1, device_id=(me, space_at(r), dp), device_id_type=MESH
+            entered, inc=1, device_id=(me, r, dp), device_id_type=MESH
         )
         return carry
 
     def send_ssq(r, carry):
         pltpu.make_async_remote_copy(
             ssq_out, ssq_in.at[sp], ssq_send, ssq_recv,
-            device_id=(me, space_at(r), dp), device_id_type=MESH,
+            device_id=(me, r, dp), device_id_type=MESH,
         ).start()
         return carry
 
@@ -152,30 +164,41 @@
     def o_target(slot, start, size):
         return o_in.at[slot, me, pl.ds(start, size)]
 
+    def moves(h, k):
+        made = [
+            jnp.logical_and(gives, jnp.logical_and(has(k), head(k) == h))
+            for gives, _, head, has, _ in gifts
+        ]
+        return jnp.logical_or(made[0], made[1])
+
     def push_main(source, target, h, send, recv):
-        for t, kind in zip(peers, kind_of):
-            moves = jnp.logical_and(late, kind == h)
-
-            @pl.when(jnp.logical_not(moves))
+        for t, k in zip(peers, kind_of):
+
+            @pl.when(jnp.logical_not(moves(h, k)))
             def _():
                 push(source(t), target, h, 0, BLOCK, (t, sp, dp), send.at[h], recv)
 
-            @pl.when(moves)
+            @pl.when(moves(h, k))
             def _():
                 push(source(t), target, h, PART, BLOCK - PART, (t, sp, dp), send.at[h], recv)
 
     def push_moved(source, target, h, send, recv, own_send):
-        @pl.when(late)
-        def _():
-            for t, kind in zip(peers, kind_of):
-
-                @pl.when(kind == h)
+        for gives, plane, head, has, slot in gifts:
+
+            @pl.when(gives)
+            def _():
+                for t, k in zip(peers, kind_of):
+
+                    @pl.when(jnp.logical_and(has(k), head(k) == h))
+                    def _():
+                        push(source(t), target, slot, 0, PART, (t, plane, dp), send.at[h], recv)
+
+                @pl.when(jnp.logical_and(has(kind), head(kind) == h))
                 def _():
-                    push(source(t), target, GUEST, 0, PART, (t, partner, dp), send.at[h], recv)
-
-            @pl.when(given == h)
-            def _():
-                push(source(me), target, GUEST, 0, PART, (me, partner, dp), own_send, recv)
+                    push(
+                        source(me), target, slot, 0, PART, (me, plane, dp),
+                        own_send.at[slot - GUEST], recv,
+                    )
 
     def qk_source(h):
         return block_source(lambda h, rows: proj.at[pl.ds(0, 2), h, rows], h)
@@ -187,7 +210,7 @@
         push_main(qk_source(h), qk_target, h, qk_send, qk_recv)
 
     def send_moved_qk(h):
-        push_moved(qk_source(h), qk_target, h, qk_send, qk_recv, guest_send.at[0])
+        push_moved(qk_source(h), qk_target, h, qk_send, qk_recv, guest_qk_send)
 
     send_qk(0)
     lax.fori_loop(0, rank, enter, 0)
@@ -239,17 +262,21 @@
     for f in range(FRAMES):
         scale[pl.ds(0, OWN_HEADS), f : f + 1, :] = steps[:, pl.ds(steps_at[f], 1), :]
 
-    @pl.when(late)
-    def _():
-        for c in range(2):
-            head_out[c : c + 1, :] = gains[c, pl.ds(given, 1), :]
-        for row in range(2, 4):
-            head_out[row : row + 1, :] = weight[pl.ds(given, 1), :]
-        head_out[4:8, :] = steps[given]
-        pltpu.make_async_remote_copy(
-            head_out, head_in, guest_send.at[1], head_recv,
-            device_id=(me, partner, dp), device_id_type=MESH,
-        ).start()
+    for gives, plane, head, has, slot in gifts:
+        guest = slot - GUEST
+
+        @pl.when(jnp.logical_and(gives, has(kind)))
+        def _():
+            row = pl.ds(head(kind), 1)
+            for c in range(2):
+                head_out[guest, c : c + 1, :] = gains[c, row, :]
+            for c in range(2, 4):
+                head_out[guest, c : c + 1, :] = weight[row, :]
+            head_out[guest, 4:8, :] = steps[head(kind)]
+            pltpu.make_async_remote_copy(
+                head_out.at[guest], head_in.at[guest], head_send.at[guest], head_recv.at[guest],
+                device_id=(me, plane, dp), device_id_type=MESH,
+            ).start()
 
     z[...] = jnp.zeros_like(z)
 
@@ -294,7 +321,7 @@
 
         lax.fori_loop(0, PIXELS // QUERY_TILE, tile, 0)
         push_main(o_source(h), o_target, h, o_send, o_recv)
-        push_moved(o_source(h), o_target, h, o_send, o_recv, guest_send.at[2])
+        push_moved(o_source(h), o_target, h, o_send, o_recv, guest_o_send)
         o_in[h, me] = o_out[h, rows_of(me), :]
         return carry
 
@@ -309,16 +336,32 @@
         for h in range(OWN_HEADS):
             qk_in[h, me, c] = own_qk[c, h]
 
-    @pl.when(late)
-    def _():
-        qk_in[given, :, :, 0:PART, :] = jnp.zeros((FRAMES, 2, PART, HEAD), jnp.bfloat16)
-        o_in[given, :, 0:PART, :] = jnp.zeros((FRAMES, PART, HEAD), jnp.bfloat16)
-
-    @pl.when(jnp.logical_not(late))
-    def _():
-        rest = BLOCK - PART
-        qk_in[GUEST, :, :, PART:BLOCK, :] = jnp.zeros((FRAMES, 2, rest, HEAD), jnp.bfloat16)
-        o_in[GUEST, :, PART:BLOCK, :] = jnp.zeros((FRAMES, rest, HEAD), jnp.bfloat16)
+    for gives, _, head, has, _ in gifts:
+
+        @pl.when(jnp.logical_and(gives, has(kind)))
+        def _():
+            none = jnp.zeros((FRAMES, PART, HEAD), jnp.bfloat16)
+            for c in range(2):
+                qk_in[head(kind), :, c, 0:PART, :] = none
+            o_in[head(kind), :, 0:PART, :] = none
+
+    for hosts, slot in ((first_host, GUEST), (second_host, GUEST + 1)):
+
+        @pl.when(hosts)
+        def _():
+            none = jnp.zeros((FRAMES, BLOCK - PART, HEAD), jnp.bfloat16)
+            for c in range(2):
+                qk_in[slot, :, c, PART:BLOCK, :] = none
+            o_in[slot, :, PART:BLOCK, :] = none
+            wait_bytes(head_in.at[slot - GUEST], head_recv.at[slot - GUEST])
+
+    for hosts, slot in ((first_host, GUEST), (second_host, GUEST + 1)):
+
+        @pl.when(hosts)
+        def _():
+            for f in range(FRAMES):
+                row = head_in[slot - GUEST, pl.ds(4 + steps_at[f], 1), :]
+                scale[slot, f : f + 1, :] = row
 
     side = FRAMES * GROUP
     at_row = lax.broadcasted_iota(jnp.int32, (side, side), 0)
@@ -327,16 +370,10 @@
     key_frame = at_lane // GROUP
     my_half = pl.ds(pl.multiple_of(half * BLOCK, BLOCK), BLOCK)
 
-    heads = OWN_HEADS + jnp.where(late, 0, 1)
-
-    @pl.when(jnp.logical_not(late))
-    def _():
-        wait_bytes(head_in, head_recv)
-        for f in range(FRAMES):
-            scale[GUEST, f : f + 1, :] = head_in[pl.ds(4 + steps_at[f], 1), :]
+    heads = OWN_HEADS + jnp.where(first_host, 1, 0) + jnp.where(second_host, 1, 0)
 
     def arrive(part, sems, h):
-        less = jnp.logical_and(late, given == h)
+        less = moves(h, kind)
 
         @pl.when(jnp.logical_and(h < GUEST, jnp.logical_not(less)))
         def _():
@@ -346,7 +383,7 @@
         def _():
             wait_bytes(part(h, FRAMES - 1, BLOCK - PART), sems.at[h])
 
-        @pl.when(h == GUEST)
+        @pl.when(h >= GUEST)
         def _():
             wait_bytes(part(h, FRAMES, PART), sems.at[h])
 
@@ -357,14 +394,15 @@
         return o_in.at[h, pl.ds(0, frames), pl.ds(0, rows)]
 
     def of_head(own, row, h):
-        return jnp.where(h < GUEST, own[pl.ds(jnp.minimum(h, GUEST - 1), 1), :], row)
+        guest = head_in[jnp.maximum(h - GUEST, 0), row : row + 1, :]
+        return jnp.where(h < GUEST, own[pl.ds(jnp.minimum(h, GUEST - 1), 1), :], guest)
 
     def temporal_weights(h, carry):
         arrive(qk_part, qk_recv, h)
         wide = []
         for c in range(2):
             part = qk_in[h, :, c].astype(jnp.float32) * fcol[c, :, my_half, :]
-            gain = of_head(gains.at[c], head_in[c : c + 1, :], h)
+            gain = of_head(gains.at[c], c, h)
             wide.append(part * gain.reshape(1, 1, HEAD))
         for b in range(GROUPS):
             queries, keys = (
@@ -393,7 +431,7 @@
         arrive(o_part, o_recv, h)
         spatial = o_in[h].astype(jnp.float32)
         row_scale = scale[h].reshape(FRAMES, 1, HEAD)
-        row_weight = of_head(weight, head_in[2:3, :], h).reshape(1, 1, HEAD)
+        row_weight = of_head(weight, 2, h).reshape(1, 1, HEAD)
         for b in range(GROUPS):
             pixels = slice(GROUP * b, GROUP * (b + 1))
             block = spatial[:, pixels, :]
@@ -443,15 +481,19 @@
         wait_bytes(qk_in.at[h, pl.ds(0, FRAMES - 1)], qk_send.at[h])
         wait_bytes(o_in.at[h, pl.ds(0, FRAMES - 1)], o_send.at[h])
 
-    @pl.when(late)
-    def _():
-        wait_bytes(qk_part(GUEST, 1, PART), guest_send.at[0])
-        wait_bytes(head_out, guest_send.at[1])
-        wait_bytes(o_part(GUEST, 1, PART), guest_send.at[2])
+    for gives, _, _, has, slot in gifts:
+        guest = slot - GUEST
+
+        @pl.when(jnp.logical_and(gives, has(kind)))
+        def _():
+            wait_bytes(qk_part(slot, 1, PART), guest_qk_send.at[guest])
+            wait_bytes(head_out.at[guest], head_send.at[guest])
+            wait_bytes(o_part(slot, 1, PART), guest_o_send.at[guest])
 
     wait_bytes(fin_out.at[pl.ds(0, FRAMES - 1)], fin_send)
     wait_bytes(fin_in, fin_recv)
-    out[...] = jnp.sum(fin_in[...], axis=0)
+    totals = jnp.sum(fin_in[...], axis=0)
+    out[...] = totals[0:1, :] * lax.rsqrt(totals[1:2, :] / CHANNELS + EPSILON)
 
 
 def on_device(projected, q_gain, k_gain, head_weight, step_scale, timestep, frame_count):
@@ -460,39 +502,39 @@
     any_space = pl.BlockSpec(memory_space=pl.ANY)
     bf16, f32 = jnp.bfloat16, jnp.float32
     dma = pltpu.SemaphoreType.DMA
-    totals = pl.pallas_call(
+    return pl.pallas_call(
         kernel,
-        out_shape=jax.ShapeDtypeStruct((2, 128), f32),
+        out_shape=jax.ShapeDtypeStruct((1, 128), f32),
         in_specs=[any_space] * 7,
         out_specs=pl.BlockSpec(memory_space=pltpu.VMEM),
         scratch_shapes=[
             pltpu.VMEM((3, OWN_HEADS, PIXELS, HEAD), bf16),
-            pltpu.VMEM((OWN_HEADS + 1, FRAMES, 2, BLOCK, HEAD), bf16),
+            pltpu.VMEM((SLOTS, FRAMES, 2, BLOCK, HEAD), bf16),
             pltpu.VMEM((2, OWN_HEADS, BLOCK, HEAD), bf16),
             pltpu.VMEM((OWN_HEADS, PIXELS, HEAD), bf16),
-            pltpu.VMEM((OWN_HEADS + 1, FRAMES, BLOCK, HEAD), bf16),
+            pltpu.VMEM((SLOTS, FRAMES, BLOCK, HEAD), bf16),
             pltpu.VMEM((ROWS, 2, 128), f32),
             pltpu.VMEM((SPACE, ROWS, 2, 128), f32),
             pltpu.VMEM((ROWS, 2, 128), f32),
             pltpu.VMEM((FRAMES, 2, 128), f32),
             pltpu.VMEM((2, OWN_HEADS, PIXELS, HEAD), bf16),
             pltpu.VMEM((2, FRAMES, 128, 128), f32),
-            pltpu.VMEM((OWN_HEADS + 1, GROUPS, 128, 128), bf16),
-            pltpu.VMEM((OWN_HEADS + 1, FRAMES, HEAD), f32),
+            pltpu.VMEM((SLOTS, GROUPS, 128, 128), bf16),
+            pltpu.VMEM((SLOTS, FRAMES, HEAD), f32),
             pltpu.VMEM((128, 128), f32),
             pltpu.VMEM((FRAMES, 2, 128), f32),
             pltpu.VMEM((FRAMES, 2, 128), f32),
             pltpu.VMEM((2, OWN_HEADS, HEAD), f32),
             pltpu.VMEM((OWN_HEADS, HEAD), f32),
             pltpu.VMEM((OWN_HEADS, STEPS, HEAD), f32),
-            pltpu.VMEM((8, HEAD), f32),
-            pltpu.VMEM((8, HEAD), f32),
+            pltpu.VMEM((2, 8, HEAD), f32),
+            pltpu.VMEM((2, 8, HEAD), f32),
             pltpu.VMEM((GROUPS, 128), jnp.int32),
             pltpu.SMEM((FRAMES,), jnp.int32),
             pltpu.SMEM((PIXELS,), jnp.int32),
-            dma((9,)), dma, dma((OWN_HEADS,)), dma((OWN_HEADS + 1,)), dma, dma, dma, dma,
-            dma((OWN_HEADS,)), dma((OWN_HEADS + 1,)), dma, dma, dma,
-            pltpu.SemaphoreType.REGULAR, dma((3,)), dma,
+            dma((9,)), dma, dma((OWN_HEADS,)), dma((SLOTS,)), dma, dma, dma, dma,
+            dma((OWN_HEADS,)), dma((SLOTS,)), dma, dma, dma,
+            pltpu.SemaphoreType.REGULAR, dma((2,)), dma((2,)), dma((2,)), dma((2,)),
         ],
         compiler_params=pltpu.CompilerParams(
             collective_id=0, has_side_effects=True, vmem_limit_bytes=56 * 2**20
@@ -502,7 +544,6 @@
         ),
         name="space_time_attention",
     )(proj, q_gain, k_gain, head_weight, steps, timestep, frame_count)
-    return totals[0:1] * lax.rsqrt(totals[1:2] / CHANNELS + EPSILON)
 
 
 def solution(mesh):

time: 69.8 us -> 68.6 us (0.983)
  other arithmetic: 1.28 us -> 0 us
  Pallas kernels: 68.4 us -> 67.2 us
  local copies, waits for them, and re-layouts: 0 us -> 1.19 us
    mul x1 -> x0, other arithmetic: 1.28 us -> none  [on_device(): return totals[0:1] * lax.rsqrt(totals[1:2] / CHANNELS + EPSILON)]
    unnamed x0 -> x1, local copies, waits for them, and re-layouts: none -> 1.19 us
    pallas_call x1, Pallas kernels: 68.4 us -> 67.2 us  [on_device(): pl.pallas_call(kernel, out_shape=jax.ShapeDtypeStruct((1, 128), f32), in_...]
where the time goes in v4:
time: 68.6 us; the launch traced here: 68.4 us
  Pallas kernels  67.2 us (98%)
  local copies, waits for them, and re-layouts  1.19 us (2%)
    pallas_call x1, Pallas kernels, on_device(): pl.pallas_call(kernel, out_shape=jax.ShapeDtypeStruct((1, 128), f32), in_...  67.2 us

profile of v4, /device:TPU:1, one launch (start us, length us, event | category | flops | bytes accessed | tf_op | source)
XLA Modules:
  0.0 68.4 jit_solution(11042860693239676197)
XLA Ops:
  0.0 67.2 %space_time_attention.1 = f32[1,128]{1,0:T(1,128)} custom-call(bf16[3,5,1024,128]{3,2,1,0:T(8,128)(2,1)} %bitcast.4, f32[5,128]{1,0:T(8,128)} %q_gain.1, f32[5,128]{1,0:T(8,128)} %k_gain.1, f32[5,128]{1,0:T(8,128)} %head_weight.1, f32[5,4,128]{2,1,0:T(4,128)} %bitcast.5, s32[16]{0:T(128)} %timestep.1, s32[1024]{0:T(1024)} %frame_count.1), custom_call_target="tpu_custom_call" | custom-call | flops 3000000000 | bytes 8000000 | tf_op jit(solution)/shard_map/space_time_attention/pallas_call | solution.py:505
  67.2 1.2 %copy.9 = f32[1,128]{1,0:T(1,128)} copy(f32[1,128]{1,0:T(1,128)} %space_time_attention.1) | data formatting | bytes 1024

commit v5 on v4

--- a/solution.py
+++ b/solution.py
@@ -24,6 +24,8 @@
 SIDE = 4
 GUEST = OWN_HEADS
 SLOTS = OWN_HEADS + 2
+LAST_PLANE = 4
+SECOND_HOST = 1
 PART = 16
 
 EPSILON = 1e-06
@@ -86,18 +88,18 @@
     kind_of = [kinds[dy][dx] for dy, dx in OFFSETS]
     kind = kinds[0][0]
     late = sp >= SPACE // 2
-    last = jnp.logical_and(late, sp < SPACE // 2 + 2)
+    last = sp == LAST_PLANE
     partner = 2 * (SPACE // 2 - 1 - sp // 2) + sp % 2
 
     def next_head(k):
         return k + 1 - jnp.where(k == SIDE - 1, SIDE, 0)
 
     gifts = (
-        (late, partner, lambda k: k, lambda k: k >= 0, GUEST),
-        (last, sp % 2, next_head, lambda k: k % 2 == 0, GUEST + 1),
+        (late, partner, lambda k: k, GUEST),
+        (last, SECOND_HOST, next_head, GUEST + 1),
     )
     first_host = jnp.logical_not(late)
-    second_host = jnp.logical_and(sp < 2, kind % 2 == 0)
+    second_host = sp == SECOND_HOST
 
     @pl.when(first_host)
     def _():
@@ -110,11 +112,11 @@
     def _():
         for t in peers:
             pl.semaphore_signal(
-                barrier, inc=1, device_id=(t, sp + SPACE // 2, dp), device_id_type=MESH
+                barrier, inc=1, device_id=(t, LAST_PLANE, dp), device_id_type=MESH
             )
 
     held = len(peers) + rank + jnp.where(late, len(peers), 0)
-    held += jnp.where(last, FRAMES // 2 - jnp.where(kind % 2 == 0, 1, 0), 0)
+    held += jnp.where(last, len(peers), 0)
 
     def announce(r, carry):
         pl.semaphore_signal(
@@ -166,8 +168,7 @@
 
     def moves(h, k):
         made = [
-            jnp.logical_and(gives, jnp.logical_and(has(k), head(k) == h))
-            for gives, _, head, has, _ in gifts
+            jnp.logical_and(gives, head(k) == h) for gives, _, head, _ in gifts
         ]
         return jnp.logical_or(made[0], made[1])
 
@@ -183,17 +184,17 @@
                 push(source(t), target, h, PART, BLOCK - PART, (t, sp, dp), send.at[h], recv)
 
     def push_moved(source, target, h, send, recv, own_send):
-        for gives, plane, head, has, slot in gifts:
+        for gives, plane, head, slot in gifts:
 
             @pl.when(gives)
             def _():
                 for t, k in zip(peers, kind_of):
 
-                    @pl.when(jnp.logical_and(has(k), head(k) == h))
+                    @pl.when(head(k) == h)
                     def _():
                         push(source(t), target, slot, 0, PART, (t, plane, dp), send.at[h], recv)
 
-                @pl.when(jnp.logical_and(has(kind), head(kind) == h))
+                @pl.when(head(kind) == h)
                 def _():
                     push(
                         source(me), target, slot, 0, PART, (me, plane, dp),
@@ -262,10 +263,10 @@
     for f in range(FRAMES):
         scale[pl.ds(0, OWN_HEADS), f : f + 1, :] = steps[:, pl.ds(steps_at[f], 1), :]
 
-    for gives, plane, head, has, slot in gifts:
+    for gives, plane, head, slot in gifts:
         guest = slot - GUEST
 
-        @pl.when(jnp.logical_and(gives, has(kind)))
+        @pl.when(gives)
         def _():
             row = pl.ds(head(kind), 1)
             for c in range(2):
@@ -336,26 +337,23 @@
         for h in range(OWN_HEADS):
             qk_in[h, me, c] = own_qk[c, h]
 
-    for gives, _, head, has, _ in gifts:
-
-        @pl.when(jnp.logical_and(gives, has(kind)))
+    for gives, _, head, _ in gifts:
+
+        @pl.when(gives)
         def _():
             none = jnp.zeros((FRAMES, PART, HEAD), jnp.bfloat16)
             for c in range(2):
                 qk_in[head(kind), :, c, 0:PART, :] = none
             o_in[head(kind), :, 0:PART, :] = none
 
-    for hosts, slot in ((first_host, GUEST), (second_host, GUEST + 1)):
+    guests = ((first_host, GUEST), (second_host, GUEST + 1))
+    for hosts, slot in guests:
 
         @pl.when(hosts)
         def _():
-            none = jnp.zeros((FRAMES, BLOCK - PART, HEAD), jnp.bfloat16)
-            for c in range(2):
-                qk_in[slot, :, c, PART:BLOCK, :] = none
-            o_in[slot, :, PART:BLOCK, :] = none
             wait_bytes(head_in.at[slot - GUEST], head_recv.at[slot - GUEST])
 
-    for hosts, slot in ((first_host, GUEST), (second_host, GUEST + 1)):
+    for hosts, slot in guests:
 
         @pl.when(hosts)
         def _():
@@ -370,22 +368,16 @@
     key_frame = at_lane // GROUP
     my_half = pl.ds(pl.multiple_of(half * BLOCK, BLOCK), BLOCK)
 
-    heads = OWN_HEADS + jnp.where(first_host, 1, 0) + jnp.where(second_host, 1, 0)
-
     def arrive(part, sems, h):
         less = moves(h, kind)
 
-        @pl.when(jnp.logical_and(h < GUEST, jnp.logical_not(less)))
+        @pl.when(jnp.logical_not(less))
         def _():
             wait_bytes(part(h, FRAMES - 1, BLOCK), sems.at[h])
 
         @pl.when(less)
         def _():
             wait_bytes(part(h, FRAMES - 1, BLOCK - PART), sems.at[h])
-
-        @pl.when(h >= GUEST)
-        def _():
-            wait_bytes(part(h, FRAMES, PART), sems.at[h])
 
     def qk_part(h, frames, rows):
         return qk_in.at[h, pl.ds(0, frames), :, pl.ds(0, rows)]
@@ -393,18 +385,13 @@
     def o_part(h, frames, rows):
         return o_in.at[h, pl.ds(0, frames), pl.ds(0, rows)]
 
-    def of_head(own, row, h):
-        guest = head_in[jnp.maximum(h - GUEST, 0), row : row + 1, :]
-        return jnp.where(h < GUEST, own[pl.ds(jnp.minimum(h, GUEST - 1), 1), :], guest)
-
-    def temporal_weights(h, carry):
-        arrive(qk_part, qk_recv, h)
+    def temporal_weights(h, count, gain):
         wide = []
         for c in range(2):
-            part = qk_in[h, :, c].astype(jnp.float32) * fcol[c, :, my_half, :]
-            gain = of_head(gains.at[c], c, h)
-            wide.append(part * gain.reshape(1, 1, HEAD))
-        for b in range(GROUPS):
+            factor = fcol[c, :, pl.ds(pl.multiple_of(half * BLOCK, BLOCK), count), :]
+            part = qk_in[h, :, c, 0:count, :].astype(jnp.float32) * factor
+            wide.append(part * gain(c).reshape(1, 1, HEAD))
+        for b in range(count // GROUP):
             queries, keys = (
                 w[:, GROUP * b : GROUP * (b + 1), :].reshape(side, HEAD).astype(jnp.bfloat16)
                 for w in wide
@@ -418,21 +405,30 @@
             exponent = jnp.exp2((scores - top) * SCALE_LOG2E)
             share = 1.0 / jnp.sum(exponent, axis=1, keepdims=True)
             mix[h, b] = (exponent * share).astype(jnp.bfloat16)
+
+    def own_weights(h, carry):
+        arrive(qk_part, qk_recv, h)
+        temporal_weights(h, BLOCK, lambda c: gains[c, pl.ds(h, 1), :])
         return carry
 
-    lax.fori_loop(0, heads, temporal_weights, 0)
+    lax.fori_loop(0, OWN_HEADS, own_weights, 0)
+    for hosts, slot in guests:
+
+        @pl.when(hosts)
+        def _():
+            wait_bytes(qk_part(slot, FRAMES, PART), qk_recv.at[slot])
+            temporal_weights(slot, PART, lambda c: head_in[slot - GUEST, c : c + 1, :])
 
     at_frame = lax.broadcasted_iota(jnp.int32, (FRAMES, GROUP, 128), 0)
     at_lane3 = lax.broadcasted_iota(jnp.int32, (FRAMES, GROUP, 128), 2)
     dot_lane = at_frame == at_lane3
     square_lane = at_frame + FRAMES == at_lane3
 
-    def temporal_head(h, carry):
-        arrive(o_part, o_recv, h)
-        spatial = o_in[h].astype(jnp.float32)
+    def temporal_head(h, count, own_weight):
+        spatial = o_in[h, :, 0:count, :].astype(jnp.float32)
         row_scale = scale[h].reshape(FRAMES, 1, HEAD)
-        row_weight = of_head(weight, 2, h).reshape(1, 1, HEAD)
-        for b in range(GROUPS):
+        row_weight = own_weight.reshape(1, 1, HEAD)
+        for b in range(count // GROUP):
             pixels = slice(GROUP * b, GROUP * (b + 1))
             block = spatial[:, pixels, :]
             mixed = jnp.dot(
@@ -445,9 +441,19 @@
             placed = jnp.where(dot_lane, dots, 0.0) + jnp.where(square_lane, squares, 0.0)
             at = pl.ds(pl.multiple_of(half * BLOCK + GROUP * b, GROUP), GROUP)
             z[at, :] += jnp.sum(placed, axis=0)
+
+    def own_head(h, carry):
+        arrive(o_part, o_recv, h)
+        temporal_head(h, BLOCK, weight[pl.ds(h, 1), :])
         return carry
 
-    lax.fori_loop(0, heads, temporal_head, 0)
+    lax.fori_loop(0, OWN_HEADS, own_head, 0)
+    for hosts, slot in guests:
+
+        @pl.when(hosts)
+        def _():
+            wait_bytes(o_part(slot, FRAMES, PART), o_recv.at[slot])
+            temporal_head(slot, PART, head_in[slot - GUEST, 2:3, :])
 
     turned = jnp.transpose(z[...])
     for f in range(FRAMES):
@@ -481,10 +487,10 @@
         wait_bytes(qk_in.at[h, pl.ds(0, FRAMES - 1)], qk_send.at[h])
         wait_bytes(o_in.at[h, pl.ds(0, FRAMES - 1)], o_send.at[h])
 
-    for gives, _, _, has, slot in gifts:
+    for gives, _, _, slot in gifts:
         guest = slot - GUEST
 
-        @pl.when(jnp.logical_and(gives, has(kind)))
+        @pl.when(gives)
         def _():
             wait_bytes(qk_part(slot, 1, PART), guest_qk_send.at[guest])
             wait_bytes(head_out.at[guest], head_send.at[guest])

time: 68.6 us -> 68 us (level)
  no operation moved by 1% of the time
where the time goes in v5:
time: 68 us; the launch traced here: 67.9 us
  Pallas kernels  66.7 us (98%)
  local copies, waits for them, and re-layouts  1.19 us (2%)
    pallas_call x1, Pallas kernels, on_device(): pl.pallas_call(kernel, out_shape=jax.ShapeDtypeStruct((1, 128), f32), in_...  66.7 us

profile of v5, /device:TPU:1, one launch (start us, length us, event | category | flops | bytes accessed | tf_op | source)
XLA Modules:
  0.0 67.9 jit_solution(13244188801183733317)
XLA Ops:
  0.0 66.7 %space_time_attention.1 = f32[1,128]{1,0:T(1,128)} custom-call(bf16[3,5,1024,128]{3,2,1,0:T(8,128)(2,1)} %bitcast.4, f32[5,128]{1,0:T(8,128)} %q_gain.1, f32[5,128]{1,0:T(8,128)} %k_gain.1, f32[5,128]{1,0:T(8,128)} %head_weight.1, f32[5,4,128]{2,1,0:T(4,128)} %bitcast.5, s32[16]{0:T(128)} %timestep.1, s32[1024]{0:T(1024)} %frame_count.1), custom_call_target="tpu_custom_call" | custom-call | flops 3000000000 | bytes 8000000 | tf_op jit(solution)/shard_map/space_time_attention/pallas_call | solution.py:511
  66.7 1.2 %copy.9 = f32[1,128]{1,0:T(1,128)} copy(f32[1,128]{1,0:T(1,128)} %space_time_attention.1) | data formatting | bytes 1024

commit v6 on v5

--- a/solution.py
+++ b/solution.py
@@ -24,6 +24,7 @@
 SIDE = 4
 GUEST = OWN_HEADS
 SLOTS = OWN_HEADS + 2
+HALF = BLOCK // 2
 LAST_PLANE = 4
 SECOND_HOST = 1
 PART = 16
@@ -54,7 +55,7 @@
     x, qk_in, own_qk, o_out, o_in, ssq_out, ssq_in, fac_out, fac_in, normed, fcol, mix, scale, z,
     fin_out, fin_in, gains, weight, steps, head_out, head_in, live, steps_at, counts,
     local_sem, own_sem, qk_send, qk_recv, ssq_send, ssq_recv, fac_send, fac_recv,
-    o_send, o_recv, fin_send, fin_recv, last_send, entered, guest_qk_send, guest_o_send, head_send, head_recv,
+    o_send, o_recv, fin_send, fin_recv, last_send, half_recv, entered, guest_qk_send, guest_o_send, head_send, head_recv,
 ):
     me = lax.axis_index("tm")
     sp = lax.axis_index("space")
@@ -321,8 +322,21 @@
             return carry
 
         lax.fori_loop(0, PIXELS // QUERY_TILE, tile, 0)
-        push_main(o_source(h), o_target, h, o_send, o_recv)
-        push_moved(o_source(h), o_target, h, o_send, o_recv, guest_o_send)
+        @pl.when(h < OWN_HEADS - 1)
+        def _():
+            push_main(o_source(h), o_target, h, o_send, o_recv)
+            push_moved(o_source(h), o_target, h, o_send, o_recv, guest_o_send)
+
+        @pl.when(h == OWN_HEADS - 1)
+        def _():
+            for start, sem in ((0, o_recv.at[OWN_HEADS - 1]), (HALF, half_recv)):
+                for t in peers:
+                    pltpu.make_async_remote_copy(
+                        o_source(OWN_HEADS - 1)(t)(start, HALF),
+                        o_target(OWN_HEADS - 1, start, HALF), o_send.at[OWN_HEADS - 1], sem,
+                        device_id=(t, sp, dp), device_id_type=MESH,
+                    ).start()
+
         o_in[h, me] = o_out[h, rows_of(me), :]
         return carry
 
@@ -424,22 +438,22 @@
     dot_lane = at_frame == at_lane3
     square_lane = at_frame + FRAMES == at_lane3
 
-    def temporal_head(h, count, own_weight):
-        spatial = o_in[h, :, 0:count, :].astype(jnp.float32)
+    def temporal_head(h, count, own_weight, start=0):
+        spatial = o_in[h, :, start : start + count, :].astype(jnp.float32)
         row_scale = scale[h].reshape(FRAMES, 1, HEAD)
         row_weight = own_weight.reshape(1, 1, HEAD)
         for b in range(count // GROUP):
             pixels = slice(GROUP * b, GROUP * (b + 1))
             block = spatial[:, pixels, :]
             mixed = jnp.dot(
-                mix[h, b], block.reshape(side, HEAD).astype(jnp.bfloat16),
+                mix[h, start // GROUP + b], block.reshape(side, HEAD).astype(jnp.bfloat16),
                 preferred_element_type=jnp.float32,
             ).astype(jnp.bfloat16).astype(jnp.float32)
             modulated = (block + mixed.reshape(FRAMES, GROUP, HEAD)) * row_scale
             dots = jnp.sum(modulated * row_weight, axis=2, keepdims=True)
             squares = jnp.sum(modulated * modulated, axis=2, keepdims=True)
             placed = jnp.where(dot_lane, dots, 0.0) + jnp.where(square_lane, squares, 0.0)
-            at = pl.ds(pl.multiple_of(half * BLOCK + GROUP * b, GROUP), GROUP)
+            at = pl.ds(pl.multiple_of(half * BLOCK + start + GROUP * b, GROUP), GROUP)
             z[at, :] += jnp.sum(placed, axis=0)
 
     def own_head(h, carry):
@@ -447,7 +461,12 @@
         temporal_head(h, BLOCK, weight[pl.ds(h, 1), :])
         return carry
 
-    lax.fori_loop(0, OWN_HEADS, own_head, 0)
+    lax.fori_loop(0, OWN_HEADS - 1, own_head, 0)
+    end = OWN_HEADS - 1
+    for start, sem in ((0, o_recv.at[end]), (HALF, half_recv)):
+        wait_bytes(o_in.at[end, pl.ds(0, FRAMES - 1), pl.ds(start, HALF)], sem)
+        temporal_head(end, HALF, weight[end : end + 1, :], start)
+
     for hosts, slot in guests:
 
         @pl.when(hosts)
@@ -540,6 +559,7 @@
             pltpu.SMEM((PIXELS,), jnp.int32),
             dma((9,)), dma, dma((OWN_HEADS,)), dma((SLOTS,)), dma, dma, dma, dma,
             dma((OWN_HEADS,)), dma((SLOTS,)), dma, dma, dma,
+            dma,
             pltpu.SemaphoreType.REGULAR, dma((2,)), dma((2,)), dma((2,)), dma((2,)),
         ],
         compiler_params=pltpu.CompilerParams(

time: 68 us -> 68.1 us (level)
  no operation moved by 1% of the time
where the time goes in v6:
time: 68.1 us; the launch traced here: 68 us
  Pallas kernels  66.8 us (98%)
  local copies, waits for them, and re-layouts  1.19 us (2%)
    pallas_call x1, Pallas kernels, on_device(): pl.pallas_call(kernel, out_shape=jax.ShapeDtypeStruct((1, 128), f32), in_...  66.8 us

profile of v6, /device:TPU:1, one launch (start us, length us, event | category | flops | bytes accessed | tf_op | source)
XLA Modules:
  0.0 68.0 jit_solution(13426028387368184762)
XLA Ops:
  0.0 66.8 %space_time_attention.1 = f32[1,128]{1,0:T(1,128)} custom-call(bf16[3,5,1024,128]{3,2,1,0:T(8,128)(2,1)} %bitcast.4, f32[5,128]{1,0:T(8,128)} %q_gain.1, f32[5,128]{1,0:T(8,128)} %k_gain.1, f32[5,128]{1,0:T(8,128)} %head_weight.1, f32[5,4,128]{2,1,0:T(4,128)} %bitcast.5, s32[16]{0:T(128)} %timestep.1, s32[1024]{0:T(1024)} %frame_count.1), custom_call_target="tpu_custom_call" | custom-call | flops 3000000000 | bytes 8000000 | tf_op jit(solution)/shard_map/space_time_attention/pallas_call | solution.py:530
  66.8 1.2 %copy.9 = f32[1,128]{1,0:T(1,128)} copy(f32[1,128]{1,0:T(1,128)} %space_time_attention.1) | data formatting | bytes 1024
